TPU v7x, 256 devices: a whole 4x4x8 slice. The times are simulated.
256 devices in a mesh: row: 8 (over x, y_hi), col: 32 (over y_lo, z, core).
Axes of the slice: x: 4, y: 4 (y_hi: 2, y_lo: 2; y = y_hi * 2 + y_lo), z: 8, core: 2. Of those that a mesh axis runs over, the one named last changes fastest.
Arguments:
- tiles: bfloat16 [12288, 256, 256], P(('row', 'col')), as said below
- tile_row: int32 [12288], P(('row', 'col')), may hold values from 0 to 255, as said below
- tile_col: int32 [12288], P(('row', 'col')), may hold values from 0 to 255, as said below
- label_class: int32 [65536], P(('row', 'col')), may hold values from -1 to 127, as said below
Outputs:
- scores: float32 [65536, 128], P(('row', 'col'))
- residual: float32 [65536, 128], P(('row', 'col'))
Inputs may be any that keep to these rules, and one draw needn't show every extreme that they name: `tiles`: Nonnegative. The tile of blocks (j, i) is the transpose of the tile of blocks (i, j); a tile on the diagonal is symmetric. No pair of blocks appears twice; the pair (j, i) is stored whenever (i, j) is. The device with row index r and col index c holds 48 tiles, all with tile_row // 32 == r and tile_col % 32 == c. `tile_col`: see tile_row. `label_class`: exactly 8192 nodes are labeled, and every class labels at least one node.
All inputs are finite; a program needn't handle non-finite values.
Results may differ from a plain program's by a relative error of at most 0.00062.
Values may be sent and summed in bfloat16 or wider, within the bound.
No kernel may reach another device: no remote copies, remote signals or barrier semaphores. Data moves between devices by JAX's collectives and lax.ppermute only.
A program may use at most 64 MiB of HBM per device.

v0:
```python
import functools

import jax
import jax.numpy as jnp
from jax import lax
from jax.sharding import Mesh
from jax.sharding import PartitionSpec as P

CLASSES = 128
ITERS = 3
ROW = ("row_0", "row_1")
COL = ("col_0", "col_1", "col_2")
ROW_COL = ("row_0", "row_1", "col_0", "col_1", "col_2")


def in_order(blocks, dim):
    shape = list(blocks.shape[1:])
    shape[dim] *= blocks.shape[0]
    return jnp.moveaxis(blocks, 0, dim).reshape(shape)


def from_everyone(array, axis):
    peers = lax.axis_size(axis)
    return lax.all_to_all(
        jnp.broadcast_to(array[None], (peers, *array.shape)), axis, 0, 0, tiled=True
    )


def collect(array, axis, dim):
    return in_order(from_everyone(array, axis), dim)


def side_by_side(arrays, axis, dim, along):
    columns = [a.reshape(*a.shape[:along], -1) for a in arrays]
    both = jnp.concatenate(columns, axis=along)
    filled, at, gathered = (lax.psum_scatter(both, axis, scatter_dimension=dim, tiled=True), 0, [])
    for a, column in zip(arrays, columns):
        section = filled[..., at : at + column.shape[along]]
        gathered.append(section.reshape(*section.shape[:along], *a.shape[along:]))
        at += column.shape[along]
    return tuple(gathered)


def split_up(array, dim, peers):
    before, after = (array.shape[:dim], array.shape[dim + 1 :])
    return jnp.moveaxis(array.reshape(*before, peers, -1, *after), dim, 0)


def summed_on_arrival(array, axis, dim):
    peers = lax.axis_size(axis)
    blocks = lax.all_to_all(split_up(array, dim, peers), axis, 0, 0, tiled=True)
    return jnp.sum(blocks, axis=0)


def over_axes(array, axes):
    return functools.reduce(lax.psum, axes, array)


def tile_apply(tiles, chosen, target, segment_count, blocks_in):
    gathered = blocks_in[chosen]
    einsum_form = "tba,tbk->tak"
    products = jnp.einsum(einsum_form, tiles, gathered, preferred_element_type=jnp.float32)
    return jax.ops.segment_sum(products, target, num_segments=segment_count)


def row_totals(tiles, target, segment_count):
    sums_axis = 1
    partial_sums = jnp.sum(tiles.astype(jnp.float32), axis=sums_axis)
    return jax.ops.segment_sum(partial_sums, target, num_segments=segment_count)


def shards(tiles, tile_row, tile_col, label_class):
    tile_size = tiles.shape[1]
    row_count = lax.axis_size(ROW)
    col_count = lax.axis_size(COL)
    in_row = tile_row % col_count
    in_col = tile_col // col_count
    unlabeled = label_class < 0
    class_axis = jnp.arange(CLASSES, dtype=jnp.int32)
    label_blocks = collect(label_class.reshape(1, tile_size), COL, 0)
    onehot = (label_blocks[:, :, None] == class_axis).astype(jnp.bfloat16)
    rhs_part = tile_apply(tiles, in_row, in_col, row_count, onehot)
    degree_part = row_totals(tiles, in_col, row_count)
    rhs_sum, degree_sum = side_by_side((rhs_part, degree_part), ROW, 0, 2)
    degree = degree_sum[0]
    rhs = jnp.where(unlabeled[:, None], rhs_sum[0], jnp.float32(0.0))
    solution = jnp.zeros((tile_size, CLASSES), jnp.float32)
    residual = rhs
    direction = rhs
    norm_now = over_axes(jnp.sum(residual * residual, axis=0), ROW_COL)
    for iteration in range(ITERS):
        panel = direction.astype(jnp.bfloat16).reshape(1, tile_size, CLASSES)
        panels = collect(panel, COL, 0)
        partial_image = tile_apply(tiles, in_row, in_col, row_count, panels)
        mixed = summed_on_arrival(partial_image, ROW, 0)[0]
        image = jnp.where(unlabeled[:, None], degree[:, None] * direction - mixed, direction)
        if iteration + 1 < ITERS:
            bending, crossed, energy = (
                over_axes(jnp.sum(direction * image, axis=0), ROW_COL),
                over_axes(jnp.sum(residual * image, axis=0), ROW_COL),
                over_axes(jnp.sum(image * image, axis=0), ROW_COL),
            )
            alpha = norm_now / bending
            norm_next = norm_now - 2.0 * alpha * crossed + alpha * alpha * energy
            solution = solution + alpha * direction
            residual = residual - alpha * image
            direction = residual + norm_next / norm_now * direction
            norm_now = norm_next
        else:
            alpha = norm_now / over_axes(jnp.sum(direction * image, axis=0), ROW_COL)
            solution = solution + alpha * direction
            residual = residual - alpha * image
    return (8.0 * CLASSES * solution, residual)


def solution(mesh):
    torus = Mesh(mesh.devices.reshape(4, 2, 2, 8, 2), ("row_0", "row_1", "col_0", "col_1", "col_2"))
    return jax.shard_map(
        shards,
        mesh=torus,
        in_specs=(P(ROW_COL, None, None), P(ROW_COL), P(ROW_COL), P(ROW_COL)),
        out_specs=(P(ROW_COL, None), P(ROW_COL, None)),
        check_vma=False,
    )
```

profile of v0, /device:TPU:1, one launch (start us, length us, event | category | flops | bytes accessed | tf_op | source)
XLA Modules:
  0.0 577.6 jit_solution(17136268512194373095)
XLA Ops:
  8.5 11.1 %all-to-all-start = ((s32[32,1,256]{2,1,0:T(1,128)}), s32[32,1,256]{2,1,0:T(1,128)S(1)}, u32[]{:S(2)}, u32[]{:S(2)}) async-start(s32[32,1,256]{2,1,0:T(1,128)} %broadcast_in_dim.40), calls=%async_computation | async-start | bytes 65536 | tf_op jit(solution)/shard_map/all_to_all | solution.py:24
  31.0 7.3 %convolution_bitcast_fusion.3 = f32[48,256,128]{1,2,0:T(8,128)} fusion(pred[48,256,128]{2,1,0:T(32,128)(4,1)S(1)} %gather_fusion, bf16[48,256,256]{2,1,0:T(8,128)(2,1)} %param.4), kind=kOutput, calls=%fused_computation.14 | convolution fusion | flops 805306368 | bytes 14155776 | tf_op jit(solution)/shard_map/tba,tbk->tak/dot_general | solution.py:62
  38.4 6.5 %copy.20 = f32[48,256,128]{2,1,0:T(8,128)} copy(f32[48,256,128]{1,2,0:T(8,128)} %convolution_bitcast_fusion.3) | data formatting | bytes 12582912 | tf_op jit(solution)/shard_map/tba,tbk->tak/dot_general | solution.py:62
  45.0 9.4 %scatter_fusion = f32[8,256,128]{2,1,0:T(8,128)S(1)} fusion(f32[8,256,128]{2,1,0:T(8,128)S(1)} %broadcast.166.clone, s32[48]{0:T(128)S(1)} %and_select_fusion.1, f32[48,256,128]{2,1,0:T(8,128)} %copy.20), kind=kCustom, calls=%fused_computation.4 | custom fusion | flops 1572864 | bytes 18874560 | tf_op jit(solution)/shard_map/scatter-add | solution.py:63
  55.9 79.5 %reduce-scatter.2.cloned.1.call-done = f32[1,256,129]{2,1,0:T(8,128)} async-done(((f32[8,256,129]{2,1,0:T(8,128)}), f32[1,256,129]{2,1,0:T(8,128)}) %reduce-scatter.2.cloned.1.call-update) | async-done | bytes 132112 | tf_op jit(solution)/shard_map/reduce_scatter | solution.py:36
  136.9 58.1 %all_to_all.35 = bf16[32,1,256,128]{3,2,1,0:T(8,128)(2,1)S(1)} all-to-all(bf16[32,1,256,128]{3,2,1,0:T(8,128)(2,1)S(1)} %broadcast_in_dim.44), channel_id=1, replica_groups=mesh['row_0'=4,'row_1'=2,'col_0'=2,'col_1'=8,'col_2'=2] {'col_0','col_1'..., dimensions={0} | all-to-all | bytes 4194304 | tf_op jit(solution)/shard_map/all_to_all | solution.py:24
  197.7 7.6 %convolution_bitcast_fusion.2 = f32[48,256,128]{1,2,0:T(8,128)} fusion(bf16[48,256,128]{2,1,0:T(8,128)(2,1)} %gather_fusion.1, bf16[48,256,256]{2,1,0:T(8,128)(2,1)} %param.4), kind=kOutput, calls=%fused_computation.13 | convolution fusion | flops 805306368 | bytes 15728640 | tf_op jit(solution)/shard_map/tba,tbk->tak/dot_general | solution.py:62
  205.3 6.6 %copy.23 = f32[48,256,128]{2,1,0:T(8,128)} copy(f32[48,256,128]{1,2,0:T(8,128)} %convolution_bitcast_fusion.2) | data formatting | bytes 12582912 | tf_op jit(solution)/shard_map/tba,tbk->tak/dot_general | solution.py:62
  213.0 13.8 %scatter_fusion.1 = f32[8,256,128]{2,1,0:T(8,128)} fusion(f32[8,256,128]{2,1,0:T(8,128)} %broadcast.166.clone.1, s32[48]{0:T(128)S(1)} %and_select_fusion.1, f32[48,256,128]{2,1,0:T(8,128)} %copy.23), kind=kCustom, calls=%fused_computation.6 | custom fusion | flops 1572864 | bytes 18874560 | tf_op jit(solution)/shard_map/scatter-add | solution.py:63
  231.6 14.1 %all-to-all-done.2 = f32[8,1,256,128]{3,2,1,0:T(8,128)S(1)} async-done(((f32[8,1,256,128]{3,2,1,0:T(8,128)}), f32[8,1,256,128]{3,2,1,0:T(8,128)S(1)}, u32[]{:S(2)}, u32[]{:S(2)}) %all-to-all-start.2) | async-done | bytes 1048608 | tf_op jit(solution)/shard_map/all_to_all | solution.py:51
  245.9 6.0 %all-reduce.3 = (f32[128]{0:T(128)S(1)}, f32[128]{0:T(128)S(1)}, f32[128]{0:T(128)S(1)}) all-reduce(f32[128]{0:T(128)S(1)} %get-tuple-element.4, f32[128]{0:T(128)S(1)} %get-tuple-element.3, f32[128]{0:T(128)S(1)} %get-tuple-element.2), channel_id=1, replica_groups=mesh['row_0'=4,'row_1'=2,'col_0'=2,'col_1'=8,'col_2'=2] {'row_0'}, use_global_device_ids=true, to_apply=%region_5.6 | all-reduce | flops 384 | bytes 3072 | tf_op jit(solution)/shard_map/psum | solution.py:56
  251.9 5.3 all-reduce.9
  262.2 13.4 %all-reduce.1 = (f32[128]{0:T(128)S(1)}, f32[128]{0:T(128)S(1)}, f32[128]{0:T(128)S(1)}) all-reduce(f32[128]{0:T(128)S(1)} %get-tuple-element.29, f32[128]{0:T(128)S(1)} %get-tuple-element.30, f32[128]{0:T(128)S(1)} %get-tuple-element.31), channel_id=1, replica_groups=mesh['row_0'=4,'row_1'=2,'col_0'=2,'col_1'=8,'col_2'=2] {'col_1'}, use_global_device_ids=true, to_apply=%region_8.9 | all-reduce | flops 384 | bytes 3072 | tf_op jit(solution)/shard_map/psum | solution.py:56
  275.6 13.3 %all-reduce.5 = (f32[128]{0:T(128)S(1)}, f32[128]{0:T(128)S(1)}, f32[128]{0:T(128)S(1)}) all-reduce(f32[128]{0:T(128)S(1)} %get-tuple-element.11, f32[128]{0:T(128)S(1)} %get-tuple-element.12, f32[128]{0:T(128)S(1)} %get-tuple-element.13), channel_id=1, replica_groups=mesh['row_0'=4,'row_1'=2,'col_0'=2,'col_1'=8,'col_2'=2] {'col_2'}, use_global_device_ids=true, to_apply=%region_9.10 | all-reduce | flops 384 | bytes 3072 | tf_op jit(solution)/shard_map/psum | solution.py:56
  289.6 53.4 %all_to_all.36 = bf16[32,1,256,128]{3,2,1,0:T(8,128)(2,1)S(1)} all-to-all(bf16[32,1,256,128]{3,2,1,0:T(8,128)(2,1)S(1)} %broadcast_in_dim.45), channel_id=1, replica_groups=mesh['row_0'=4,'row_1'=2,'col_0'=2,'col_1'=8,'col_2'=2] {'col_0','col_1'..., dimensions={0} | all-to-all | bytes 4194304 | tf_op jit(solution)/shard_map/all_to_all | solution.py:24
  345.7 7.6 %convolution_bitcast_fusion.1 = f32[48,256,128]{1,2,0:T(8,128)} fusion(bf16[48,256,128]{2,1,0:T(8,128)(2,1)} %gather_fusion.2, bf16[48,256,256]{2,1,0:T(8,128)(2,1)} %param.4), kind=kOutput, calls=%fused_computation.12 | convolution fusion | flops 805306368 | bytes 15728640 | tf_op jit(solution)/shard_map/tba,tbk->tak/dot_general | solution.py:62
  353.3 6.5 %copy.26 = f32[48,256,128]{2,1,0:T(8,128)} copy(f32[48,256,128]{1,2,0:T(8,128)} %convolution_bitcast_fusion.1) | data formatting | bytes 12582912 | tf_op jit(solution)/shard_map/tba,tbk->tak/dot_general | solution.py:62
  359.9 9.4 %scatter_fusion.2 = f32[8,256,128]{2,1,0:T(8,128)S(1)} fusion(f32[8,256,128]{2,1,0:T(8,128)S(1)} %broadcast.166.clone.2, s32[48]{0:T(128)S(1)} %and_select_fusion.1, f32[48,256,128]{2,1,0:T(8,128)} %copy.26), kind=kCustom, calls=%fused_computation.7 | custom fusion | flops 1572864 | bytes 18874560 | tf_op jit(solution)/shard_map/scatter-add | solution.py:63
  369.3 16.6 %all_to_all.38 = f32[8,1,256,128]{3,2,1,0:T(8,128)S(1)} all-to-all(f32[8,1,256,128]{3,2,1,0:T(8,128)S(1)} %bitcast.53), channel_id=1, replica_groups=mesh['row_0'=4,'row_1'=2,'col_0'=2,'col_1'=8,'col_2'=2] {'row_0','row_1'}, dimensions={0} | all-to-all | bytes 2097152 | tf_op jit(solution)/shard_map/all_to_all | solution.py:51
  386.1 7.1 %all-reduce.2 = (f32[128]{0:T(128)S(1)}, f32[128]{0:T(128)S(1)}, f32[128]{0:T(128)S(1)}) all-reduce(f32[128]{0:T(128)S(1)} %get-tuple-element.6, f32[128]{0:T(128)S(1)} %get-tuple-element.7, f32[128]{0:T(128)S(1)} %get-tuple-element.5), channel_id=1, replica_groups=mesh['row_0'=4,'row_1'=2,'col_0'=2,'col_1'=8,'col_2'=2] {'row_0'}, use_global_device_ids=true, to_apply=%region_39.40 | all-reduce | flops 384 | bytes 3072 | tf_op jit(solution)/shard_map/psum | solution.py:56
  393.2 5.3 all-reduce.8
  402.8 13.8 %all-reduce = (f32[128]{0:T(128)S(1)}, f32[128]{0:T(128)S(1)}, f32[128]{0:T(128)S(1)}) all-reduce(f32[128]{0:T(128)S(1)} %get-tuple-element.26, f32[128]{0:T(128)S(1)} %get-tuple-element.27, f32[128]{0:T(128)S(1)} %get-tuple-element.28), channel_id=1, replica_groups=mesh['row_0'=4,'row_1'=2,'col_0'=2,'col_1'=8,'col_2'=2] {'col_1'}, use_global_device_ids=true, to_apply=%region_42.43 | all-reduce | flops 384 | bytes 3072 | tf_op jit(solution)/shard_map/psum | solution.py:56
  416.6 13.1 %all-reduce.4 = (f32[128]{0:T(128)S(1)}, f32[128]{0:T(128)S(1)}, f32[128]{0:T(128)S(1)}) all-reduce(f32[128]{0:T(128)S(1)} %get-tuple-element.8, f32[128]{0:T(128)S(1)} %get-tuple-element.9, f32[128]{0:T(128)S(1)} %get-tuple-element.10), channel_id=1, replica_groups=mesh['row_0'=4,'row_1'=2,'col_0'=2,'col_1'=8,'col_2'=2] {'col_2'}, use_global_device_ids=true, to_apply=%region_43.44 | all-reduce | flops 384 | bytes 3072 | tf_op jit(solution)/shard_map/psum | solution.py:56
  430.3 53.1 %all_to_all.37 = bf16[32,1,256,128]{3,2,1,0:T(8,128)(2,1)S(1)} all-to-all(bf16[32,1,256,128]{3,2,1,0:T(8,128)(2,1)S(1)} %broadcast_in_dim.46), channel_id=1, replica_groups=mesh['row_0'=4,'row_1'=2,'col_0'=2,'col_1'=8,'col_2'=2] {'col_0','col_1'..., dimensions={0} | all-to-all | bytes 4194304 | tf_op jit(solution)/shard_map/all_to_all | solution.py:24
  486.1 7.6 %convolution_bitcast_fusion = f32[48,256,128]{1,2,0:T(8,128)} fusion(bf16[48,256,128]{2,1,0:T(8,128)(2,1)} %gather_fusion.3, bf16[48,256,256]{2,1,0:T(8,128)(2,1)} %param.4), kind=kOutput, calls=%fused_computation.11 | convolution fusion | flops 805306368 | bytes 15728640 | tf_op jit(solution)/shard_map/tba,tbk->tak/dot_general | solution.py:62
  493.7 6.5 %copy.29 = f32[48,256,128]{2,1,0:T(8,128)} copy(f32[48,256,128]{1,2,0:T(8,128)} %convolution_bitcast_fusion) | data formatting | bytes 12582912 | tf_op jit(solution)/shard_map/tba,tbk->tak/dot_general | solution.py:62
  500.3 9.4 %scatter_fusion.3 = f32[8,256,128]{2,1,0:T(8,128)S(1)} fusion(f32[8,256,128]{2,1,0:T(8,128)S(1)} %broadcast.166, s32[48]{0:T(128)S(1)} %and_select_fusion.1, f32[48,256,128]{2,1,0:T(8,128)} %copy.29), kind=kCustom, calls=%fused_computation.8 | custom fusion | flops 1572864 | bytes 18874560 | tf_op jit(solution)/shard_map/scatter-add | solution.py:63
  509.7 16.1 %all_to_all.39 = f32[8,1,256,128]{3,2,1,0:T(8,128)S(1)} all-to-all(f32[8,1,256,128]{3,2,1,0:T(8,128)S(1)} %bitcast.52), channel_id=1, replica_groups=mesh['row_0'=4,'row_1'=2,'col_0'=2,'col_1'=8,'col_2'=2] {'row_0','row_1'}, dimensions={0} | all-to-all | bytes 2097152 | tf_op jit(solution)/shard_map/all_to_all | solution.py:51
  526.0 6.9 %psum.290 = f32[128]{0:T(128)S(1)} all-reduce(f32[128]{0:T(128)S(1)} %multiply_reduce_fusion), channel_id=1, replica_groups=mesh['row_0'=4,'row_1'=2,'col_0'=2,'col_1'=8,'col_2'=2] {'row_0'}, use_global_device_ids=true, to_apply=%region_47.48 | all-reduce | flops 128 | bytes 1024 | tf_op jit(solution)/shard_map/psum | solution.py:56
  533.0 5.3 psum.291
  543.5 13.3 %psum.293 = f32[128]{0:T(128)S(1)} all-reduce(f32[128]{0:T(128)S(1)} %psum.292), channel_id=1, replica_groups=mesh['row_0'=4,'row_1'=2,'col_0'=2,'col_1'=8,'col_2'=2] {'col_1'}, use_global_device_ids=true, to_apply=%region_50.51 | all-reduce | flops 128 | bytes 1024 | tf_op jit(solution)/shard_map/psum | solution.py:56
  556.8 13.1 %psum.294 = f32[128]{0:T(128)S(1)} all-reduce(f32[128]{0:T(128)S(1)} %psum.293), channel_id=1, replica_groups=mesh['row_0'=4,'row_1'=2,'col_0'=2,'col_1'=8,'col_2'=2] {'col_2'}, use_global_device_ids=true, to_apply=%region_51.52 | all-reduce | flops 128 | bytes 1024 | tf_op jit(solution)/shard_map/psum | solution.py:56
  (49 shorter events, 47.2 us)
Async XLA Ops:
  8.5 19.1 %all-to-all-start = ((s32[32,1,256]{2,1,0:T(1,128)}), s32[32,1,256]{2,1,0:T(1,128)S(1)}, u32[]{:S(2)}, u32[]{:S(2)}) async-start(s32[32,1,256]{2,1,0:T(1,128)} %broadcast_in_dim.40), calls=%async_computation | async-start | bytes 65536 | tf_op jit(solution)/shard_map/all_to_all | solution.py:24
  19.6 115.8 %reduce-scatter.2.cloned.1.call-start = ((), (), s32[]{:S(2)}) async-start(), calls=%async_computation.8 | async-start | bytes 2359296 | tf_op jit(solution)/shard_map/reduce_scatter | solution.py:36
  44.9 9.4 %copy-start = (f32[8,256,1]{2,1,0:T(8,128)S(1)}, f32[8,256,1]{2,1,0:T(8,128)}, u32[]{:S(2)}) copy-start(f32[8,256,1]{2,1,0:T(8,128)} %copy.21) | copy-start | bytes 24580
  54.4 1.5 copy-start.2
  213.0 18.6 %copy-start.1 = (f32[1,256,129]{2,1,0:T(8,128)S(1)}, f32[1,256,129]{2,1,0:T(8,128)}, u32[]{:S(2)}) copy-start(f32[1,256,129]{2,1,0:T(8,128)} %reduce-scatter.2.cloned.1.call-done) | copy-start | bytes 396292
  226.8 18.9 %all-to-all-start.2 = ((f32[8,1,256,128]{3,2,1,0:T(8,128)}), f32[8,1,256,128]{3,2,1,0:T(8,128)S(1)}, u32[]{:S(2)}, u32[]{:S(2)}) async-start(f32[8,1,256,128]{3,2,1,0:T(8,128)} %bitcast.6), calls=%async_computation.3 | async-start | bytes 2097152 | tf_op jit(solution)/shard_map/all_to_all | solution.py:51
Sparse Core Ops, SparseCore 0:
  56.0 79.3 reduce-scatter.1
where the time goes:
time: 579 us; the launch traced here: 578 us
  blocking collectives  328 us (57%)
  waiting for transfers between devices  93.8 us (16%)
  other arithmetic  53.7 us (9%)
  local copies, waits for them, and re-layouts  42 us (7%)
  matrix products  30.1 us (5%)
  starting transfers between devices  15.9 us (3%)
  between operations  14.2 us (2%)
    all_to_all x3, blocking collectives, from_everyone(): lax.all_to_all(jnp.broadcast_to(array[None], (peers, *array.shape)), axis...  165 us
    psum x15, blocking collectives, over_axes(): return functools.reduce(lax.psum, axes, array)  131 us
    reduce_scatter x1, waiting for transfers between devices, side_by_side(): lax.psum_scatter(both, axis, scatter_dimension=dim, tiled=True)  79.5 us
    scatter-add x4, other arithmetic, tile_apply(): return jax.ops.segment_sum(products, target, num_segments=segment_count)  42 us
    all_to_all x2, blocking collectives, summed_on_arrival(): blocks = lax.all_to_all(split_up(array, dim, peers), axis, 0, 0, tiled=True)  32.7 us
    dot_general x4, matrix products, tile_apply(): jnp.einsum(einsum_form, tiles, gathered, preferred_element_type=jnp.float32)  30.1 us
    dot_general x4, local copies, waits for them, and re-layouts, tile_apply(): jnp.einsum(einsum_form, tiles, gathered, preferred_element_type=jnp.float32)  26.2 us
    all_to_all x1, waiting for transfers between devices, summed_on_arrival(): blocks = lax.all_to_all(split_up(array, dim, peers), axis, 0, 0, tiled=True)  14.1 us
  transfers between devices with their start and end apart: 3, of which 3 were waited for; matrix products, arithmetic and copies ran while one was open for 1% of the time, Pallas kernels for 0%

commit v1 on v0

v1 whole, which is shorter than its diff:
```python
import functools

import jax
import jax.numpy as jnp
from jax import lax
from jax.experimental import pallas as pl
from jax.experimental.pallas import tpu as pltpu
from jax.sharding import Mesh
from jax.sharding import PartitionSpec as P

CLASSES = 128
ITERS = 3
AXES = ("x", "yh", "yl", "z", "core")
ROW = ("x", "yh")
COL = ("yl", "z", "core")
F32 = jnp.float32
BF16 = jnp.bfloat16
CHUNK = 8
PARAMS = pltpu.CompilerParams(vmem_limit_bytes=40 * 1024 * 1024)
VMEM = pl.BlockSpec(memory_space=pltpu.VMEM)
SMEM = pl.BlockSpec(memory_space=pltpu.SMEM)


def shape(dims, dtype=F32):
    return jax.ShapeDtypeStruct(dims, dtype)


def to_everyone(copies, axis):
    return lax.all_to_all(copies, axis, 0, 0, tiled=True)


def shift(array, axis, by):
    size = lax.axis_size(axis)
    return lax.ppermute(array, axis, [(i, (i + by) % size) for i in range(size)])


def accumulate(rows, panel_of, source_ref, target_ref, tiles_ref, parts, total):
    step = pl.program_id(0)

    @pl.when(step == 0)
    def _():
        total[...] = jnp.zeros_like(total)

    for t in range(CHUNK):
        at = step * CHUNK + t
        product = jnp.dot(
            panel_of(source_ref[at]), tiles_ref[t], preferred_element_type=F32
        )
        total[target_ref[at]] += product[:rows]

    @pl.when(step == pl.num_programs(0) - 1)
    def _():
        for k, part in enumerate(parts):
            part[...] = total[2 * k : 2 * k + 2]


def label_kernel(source_ref, target_ref, label_ref, tiles_ref, *rest):
    *parts, total = rest
    size = tiles_ref.shape[1]
    classes = lax.broadcasted_iota(jnp.int32, (CLASSES, size), 0)

    def panel_of(source):
        hot = jnp.where(label_ref[source] == classes, F32(1.0), F32(0.0))
        return jnp.concatenate([hot, jnp.ones((16, size), F32)], axis=0).astype(BF16)

    accumulate(CLASSES + 8, panel_of, source_ref, target_ref, tiles_ref, parts, total)


def panel_kernel(source_ref, target_ref, own_ref, other_ref, tiles_ref, *rest):
    *parts, total = rest
    half = own_ref.shape[0]

    def panel_of(source):
        at = lax.rem(source, half)
        return jnp.where(source < half, own_ref[at], other_ref[at])

    accumulate(CLASSES, panel_of, source_ref, target_ref, tiles_ref, parts, total)


def apply_tiles(kernel, rows, source, target, tiles, *panels):
    count, size, _ = tiles.shape
    whole = [pl.BlockSpec(p.shape, lambda g, n=p.ndim: (0,) * n) for p in panels]
    part = shape((2, rows, size))
    return pl.pallas_call(
        kernel,
        grid=(count // CHUNK,),
        in_specs=[SMEM, SMEM, *whole, pl.BlockSpec((CHUNK, size, size), lambda g: (g, 0, 0))],
        out_specs=[pl.BlockSpec(part.shape, lambda g: (0, 0, 0))] * 4,
        out_shape=[part] * 4,
        scratch_shapes=[pltpu.VMEM((8, rows, size), F32)],
        compiler_params=PARAMS,
    )(source, target, *panels, tiles)


def second_kernel(a_ref, b_ref, c_ref, d_ref, out_ref):
    out_ref[...] = (a_ref[1] + b_ref[1]) + (c_ref[1] + d_ref[1])


def reduce_parts(parts):
    arrived = [parts[0], *(shift(parts[k], "x", k) for k in range(1, 4))]
    second = pl.pallas_call(
        second_kernel,
        in_specs=[VMEM] * 4,
        out_specs=VMEM,
        out_shape=shape(parts[0].shape[1:]),
        compiler_params=PARAMS,
    )(*arrived)
    return (*arrived, shift(second, "yh", 1))


def sums_to_rows(sums):
    size = sums[0].shape[0]
    lane = lax.broadcasted_iota(jnp.int32, (size, CLASSES), 1)
    table = jnp.zeros((size, CLASSES), F32)
    for i, column in enumerate(sums):
        table = jnp.where(lane == i, column, table)
    return table.T[:8]


def rows_to_columns(row):
    return jnp.broadcast_to(row, (CLASSES, CLASSES)).T[:, :1]


def merged(a_ref, b_ref, c_ref, d_ref, e_ref):
    return (a_ref[0] + b_ref[0]) + (c_ref[0] + d_ref[0]) + e_ref[...]


def start_kernel(a_ref, b_ref, c_ref, d_ref, e_ref, label_ref, rhs_ref, panel_ref, degree_ref):
    mixed = merged(a_ref, b_ref, c_ref, d_ref, e_ref)
    rhs = jnp.where(label_ref[...] < 0, mixed[:CLASSES], F32(0.0))
    rhs_ref[...] = rhs
    panel_ref[...] = rhs.astype(BF16)
    degree_ref[...] = mixed[CLASSES : CLASSES + 1]


def image_kernel(
    a_ref, b_ref, c_ref, d_ref, e_ref, label_ref, degree_ref, direction_ref, residual_ref,
    image_ref, sums_ref,
):
    mixed = merged(a_ref, b_ref, c_ref, d_ref, e_ref)
    direction = direction_ref[...]
    residual = residual_ref[...]
    image = jnp.where(label_ref[...] < 0, degree_ref[...] * direction - mixed, direction)
    image_ref[...] = image
    rows = sums_to_rows(
        [
            jnp.sum(term, axis=1, keepdims=True)
            for term in (direction * image, residual * image, image * image, residual * residual)
        ]
    )
    for i in range(sums_ref.shape[0]):
        sums_ref[i] = rows


def relay_kernel(in_ref, out_ref):
    rows = jnp.sum(in_ref[...], axis=0)
    for i in range(out_ref.shape[0]):
        out_ref[i] = rows


def step_kernel(
    first, sums_ref, norm_ref, solution_ref, residual_ref, direction_ref, image_ref,
    solution_out, residual_out, direction_out, panel_out, norm_out,
):
    sums = jnp.sum(sums_ref[...], axis=0)
    bending, crossed, energy = sums[0:1], sums[1:2], sums[2:3]
    norm = sums[3:4] if first else norm_ref[...]
    alpha = norm / bending
    norm_next = norm - 2.0 * alpha * crossed + alpha * alpha * energy
    norm_out[...] = norm_next
    beta = rows_to_columns(norm_next / norm)
    alpha = rows_to_columns(alpha)
    direction = direction_ref[...]
    step = alpha * direction
    solution_out[...] = step if first else solution_ref[...] + step
    residual = residual_ref[...] - alpha * image_ref[...]
    residual_out[...] = residual
    direction = residual + beta * direction
    direction_out[...] = direction
    panel_out[...] = direction.astype(BF16)


def last_kernel(
    sums_ref, norm_ref, solution_ref, residual_ref, direction_ref, image_ref,
    scores_out, residual_out,
):
    sums = jnp.sum(sums_ref[...], axis=0)
    alpha = rows_to_columns(norm_ref[...] / sums[0:1])
    total = solution_ref[...] + alpha * direction_ref[...]
    scores_out[...] = (8.0 * CLASSES * total).T
    residual_out[...] = (residual_ref[...] - alpha * image_ref[...]).T


def call(kernel, out_shape, *args):
    return pl.pallas_call(
        kernel,
        in_specs=[VMEM] * len(args),
        out_specs=jax.tree.map(lambda _: VMEM, out_shape),
        out_shape=out_shape,
        compiler_params=PARAMS,
    )(*args)


def gather_panels(panel):
    own = lax.all_gather(panel, "z")
    own = lax.all_gather(own, "yl")
    own = own.reshape(-1, *panel.shape)
    return own, shift(own, "core", 1)


def shards(tiles, tile_row, tile_col, label_class):
    size = tiles.shape[1]
    rows = lax.axis_size(ROW)
    cols = lax.axis_size(COL)
    wide = cols // 2
    local = tile_row % cols
    mine = local % 2 == lax.axis_index("core")
    source = local // 2 + jnp.where(mine, 0, wide)
    block = tile_col // cols
    to_x = (block // 2 - lax.axis_index("x")) % 4
    to_y = (block % 2 - lax.axis_index("yh")) % 2
    target = to_x * 2 + to_y
    label = label_class.reshape(1, size)
    labels = to_everyone(jnp.broadcast_to(label[None], (cols, 1, size)), COL)
    parts = apply_tiles(label_kernel, CLASSES + 8, local, target, tiles, labels)
    field = shape((CLASSES, size))
    half = shape((CLASSES, size), BF16)
    residual, panel, degree = call(
        start_kernel, (field, half, shape((1, size))), *reduce_parts(parts), label
    )
    direction = residual
    solution = residual
    norm = jnp.zeros((1, CLASSES), F32)
    for iteration in range(ITERS):
        parts = apply_tiles(panel_kernel, CLASSES, source, target, tiles, *gather_panels(panel))
        image, sums = call(
            image_kernel,
            (field, shape((rows, 8, CLASSES))),
            *reduce_parts(parts), label, degree, direction, residual,
        )
        sums = to_everyone(sums, ROW)
        sums = call(relay_kernel, shape((cols, 8, CLASSES)), sums)
        sums = to_everyone(sums, COL)
        state = (sums, norm, solution, residual, direction, image)
        if iteration + 1 < ITERS:
            solution, residual, direction, panel, norm = call(
                functools.partial(step_kernel, iteration == 0),
                (field, field, field, half, shape((1, CLASSES))),
                *state,
            )
        else:
            out = shape((size, CLASSES))
            return call(last_kernel, (out, out), *state)


def solution(mesh):
    torus = Mesh(mesh.devices.reshape(4, 2, 2, 8, 2), AXES)
    return jax.shard_map(
        shards,
        mesh=torus,
        in_specs=(P(AXES, None, None), P(AXES), P(AXES), P(AXES)),
        out_specs=(P(AXES, None), P(AXES, None)),
        check_vma=False,
    )
```

time: 579 us -> 402 us (0.69)
  blocking collectives: 328 us -> 161 us
  waiting for transfers between devices: 93.8 us -> 153 us
  other arithmetic: 53.7 us -> 0.7 us
  matrix products: 30.1 us -> 0 us
  starting transfers between devices: 15.9 us -> 42.9 us
  local copies, waits for them, and re-layouts: 42 us -> 16.2 us
  Pallas kernels: 0 us -> 13.5 us
    psum x15 -> x0, blocking collectives: 131 us -> none  [over_axes(): return functools.reduce(lax.psum, axes, array)]
    all_to_all x5 -> x6, blocking collectives: 197 us -> 96.3 us  [to_everyone(): return lax.all_to_all(copies, axis, 0, 0, tiled=True)]
    all_gather x0 -> x3, waiting for transfers between devices: none -> 84.5 us  [gather_panels(): own = lax.all_gather(own, 'yl')]
    reduce_scatter x1 -> x0, waiting for transfers between devices: 79.5 us -> none  [side_by_side(): lax.psum_scatter(both, axis, scatter_dimension=dim, tiled=True)]
    all_gather x0 -> x3, blocking collectives: none -> 65 us  [gather_panels(): own = lax.all_gather(panel, 'z')]
    ppermute x0 -> x19, waiting for transfers between devices: none -> 61.2 us  [shift(): lax.ppermute(array, axis, [(i, (i + by) % size) for i in range(size)])]
    scatter-add x5 -> x0, other arithmetic: 42.8 us -> none  [the longest x4 42 us: tile_apply(): return jax.ops.segment_sum(products, target, num_segments=segment_count)]
    ppermute x0 -> x19, starting transfers between devices: none -> 31.6 us  [shift(): lax.ppermute(array, axis, [(i, (i + by) % size) for i in range(size)])]
  transfers between devices with their start and end apart: 3 -> 23, of which waited for: 3 -> 19; matrix products, arithmetic and copies ran while one was open for 1% -> 0% of each run, Pallas kernels for 0% -> 0%
where the time goes in v1:
time: 402 us; the launch traced here: 401 us
  blocking collectives  161 us (40%)
  waiting for transfers between devices  153 us (38%)
  starting transfers between devices  42.9 us (11%)
  local copies, waits for them, and re-layouts  16.2 us (4%)
  between operations  13.9 us (3%)
  Pallas kernels  13.5 us (3%)
    all_to_all x6, blocking collectives, to_everyone(): return lax.all_to_all(copies, axis, 0, 0, tiled=True)  96.3 us
    all_gather x3, waiting for transfers between devices, gather_panels(): own = lax.all_gather(own, 'yl')  84.5 us
    all_gather x3, blocking collectives, gather_panels(): own = lax.all_gather(panel, 'z')  65 us
    ppermute x19, waiting for transfers between devices, shift(): lax.ppermute(array, axis, [(i, (i + by) % size) for i in range(size)])  61.2 us
    ppermute x19, starting transfers between devices, shift(): lax.ppermute(array, axis, [(i, (i + by) % size) for i in range(size)])  31.6 us
    unnamed x16, local copies, waits for them, and re-layouts  14.8 us
    pallas_call x4, Pallas kernels, apply_tiles(): pl.pallas_call(kernel, grid=(count // CHUNK,), in_specs=[SMEM, SMEM, *who...  11.3 us
    all_to_all x1, starting transfers between devices, to_everyone(): return lax.all_to_all(copies, axis, 0, 0, tiled=True)  11.1 us
  transfers between devices with their start and end apart: 23, of which 19 were waited for; matrix products, arithmetic and copies ran while one was open for 0% of the time, Pallas kernels for 0%

profile of v1, /device:TPU:1, one launch (start us, length us, event | category | flops | bytes accessed | tf_op | source)
XLA Modules:
  0.0 401.4 jit_solution(13141156351411277795)
XLA Ops:
  8.5 11.1 %all-to-all-start = ((s32[32,1,256]{2,1,0:T(1,128)}), s32[32,1,256]{2,1,0:T(1,128)S(1)}, u32[]{:S(2)}, u32[]{:S(2)}) async-start(s32[32,1,256]{2,1,0:T(1,128)} %broadcast_in_dim.15), calls=%async_computation | async-start | bytes 65536 | tf_op jit(solution)/shard_map/all_to_all | solution.py:29
  20.4 7.2 %all-to-all-done.label_ref = s32[32,1,256]{2,1,0:T(1,128)S(1)} async-done(((s32[32,1,256]{2,1,0:T(1,128)}), s32[32,1,256]{2,1,0:T(1,128)S(1)}, u32[]{:S(2)}, u32[]{:S(2)}) %all-to-all-start) | async-done | bytes 32800 | tf_op jit(solution)/shard_map/all_to_all | solution.py:29
  27.6 2.8 copy-done
  30.4 2.9 shard_map.59
  38.1 3.7 collective-permute-done.b_ref
  41.8 7.0 %collective-permute-done.1.c_ref = f32[2,136,256]{2,1,0:T(8,128)S(1)} collective-permute-done((f32[2,136,256]{2,1,0:T(8,128)S(1)}, f32[2,136,256]{2,1,0:T(8,128)S(1)}, u32[]{:S(2)}, u32[]{:S(2)}) %collective-permute-start.1) | collective-permute-done | bytes 278560 | tf_op jit(solution)/shard_map/ppermute | solution.py:34
  51.5 2.8 collective-permute-done.3.e_ref
  54.3 21.9 %all-gather = bf16[1024,256]{1,0:T(8,128)(2,1)} all-gather(bf16[128,256]{1,0:T(8,128)(2,1)S(1)} %get-tuple-element.41), channel_id=2, replica_groups=mesh['x'=4,'yh'=2,'yl'=2,'z'=8,'core'=2] {'z'}, dimensions={0}, use_global_device_ids=true | all-gather | bytes 589824 | tf_op jit(solution)/shard_map/all_gather | solution.py:205
  76.3 31.5 %all-gather.10.cloned.1.call-done.own_ref = bf16[16,128,256]{2,1,0:T(8,128)(2,1)} async-done(((bf16[8,128,256]{2,1,0:T(8,128)(2,1)}), bf16[16,128,256]{2,1,0:T(8,128)(2,1)}) %all-gather.10.cloned.1.call-update) | async-done | bytes 1048592 | tf_op jit(solution)/shard_map/all_gather | solution.py:206
  111.0 2.8 copy-done.1
  115.0 2.8 shard_map.62
  122.7 3.9 collective-permute-done.5.b_ref
  126.6 6.6 %collective-permute-done.6.c_ref = f32[2,128,256]{2,1,0:T(8,128)S(1)} collective-permute-done((f32[2,128,256]{2,1,0:T(8,128)S(1)}, f32[2,128,256]{2,1,0:T(8,128)S(1)}, u32[]{:S(2)}, u32[]{:S(2)}) %collective-permute-start.6) | collective-permute-done | bytes 262176 | tf_op jit(solution)/shard_map/ppermute | solution.py:34
  135.7 2.9 collective-permute-done.8.e_ref
  138.8 13.3 %all_to_all.35.in_ref = f32[8,8,128]{2,1,0:T(8,128)S(1)} all-to-all(f32[8,8,128]{2,1,0:T(8,128)S(1)} %get-tuple-element.48), channel_id=1, replica_groups=mesh['x'=4,'yh'=2,'yl'=2,'z'=8,'core'=2] {'x','yh'}, dimensions={0} | all-to-all | bytes 65536 | tf_op jit(solution)/shard_map/all_to_all | solution.py:29
  152.1 18.8 %all_to_all.36.sums_ref = f32[32,8,128]{2,1,0:T(8,128)S(1)} all-to-all(f32[32,8,128]{2,1,0:T(8,128)S(1)} %shard_map.65), channel_id=1, replica_groups=mesh['x'=4,'yh'=2,'yl'=2,'z'=8,'core'=2] {'yl','z','core'}, dimensions={0} | all-to-all | bytes 262144 | tf_op jit(solution)/shard_map/all_to_all | solution.py:29
  171.2 21.5 %all-gather.2 = bf16[1024,256]{1,0:T(8,128)(2,1)} all-gather(bf16[128,256]{1,0:T(8,128)(2,1)S(1)} %get-tuple-element.50), channel_id=4, replica_groups=mesh['x'=4,'yh'=2,'yl'=2,'z'=8,'core'=2] {'z'}, dimensions={0}, use_global_device_ids=true | all-gather | bytes 589824 | tf_op jit(solution)/shard_map/all_gather | solution.py:205
  192.8 26.5 %all-gather.12.cloned.1.call-done.own_ref = bf16[16,128,256]{2,1,0:T(8,128)(2,1)} async-done(((bf16[8,128,256]{2,1,0:T(8,128)(2,1)}), bf16[16,128,256]{2,1,0:T(8,128)(2,1)}) %all-gather.12.cloned.1.call-update) | async-done | bytes 1048592 | tf_op jit(solution)/shard_map/all_gather | solution.py:206
  226.5 2.8 shard_map.67
  234.1 3.9 collective-permute-done.10.b_ref
  238.1 6.6 %collective-permute-done.11.c_ref = f32[2,128,256]{2,1,0:T(8,128)S(1)} collective-permute-done((f32[2,128,256]{2,1,0:T(8,128)S(1)}, f32[2,128,256]{2,1,0:T(8,128)S(1)}, u32[]{:S(2)}, u32[]{:S(2)}) %collective-permute-start.11) | collective-permute-done | bytes 262176 | tf_op jit(solution)/shard_map/ppermute | solution.py:34
  247.2 2.9 collective-permute-done.13.e_ref
  250.3 13.3 %all_to_all.37.in_ref = f32[8,8,128]{2,1,0:T(8,128)S(1)} all-to-all(f32[8,8,128]{2,1,0:T(8,128)S(1)} %get-tuple-element.57), channel_id=1, replica_groups=mesh['x'=4,'yh'=2,'yl'=2,'z'=8,'core'=2] {'x','yh'}, dimensions={0} | all-to-all | bytes 65536 | tf_op jit(solution)/shard_map/all_to_all | solution.py:29
  263.6 18.8 %all_to_all.38.sums_ref = f32[32,8,128]{2,1,0:T(8,128)S(1)} all-to-all(f32[32,8,128]{2,1,0:T(8,128)S(1)} %shard_map.70), channel_id=1, replica_groups=mesh['x'=4,'yh'=2,'yl'=2,'z'=8,'core'=2] {'yl','z','core'}, dimensions={0} | all-to-all | bytes 262144 | tf_op jit(solution)/shard_map/all_to_all | solution.py:29
  282.6 21.5 %all-gather.4 = bf16[1024,256]{1,0:T(8,128)(2,1)} all-gather(bf16[128,256]{1,0:T(8,128)(2,1)S(1)} %get-tuple-element.61), channel_id=6, replica_groups=mesh['x'=4,'yh'=2,'yl'=2,'z'=8,'core'=2] {'z'}, dimensions={0}, use_global_device_ids=true | all-gather | bytes 589824 | tf_op jit(solution)/shard_map/all_gather | solution.py:205
  304.2 26.6 %all-gather.14.cloned.1.call-done.own_ref = bf16[16,128,256]{2,1,0:T(8,128)(2,1)} async-done(((bf16[8,128,256]{2,1,0:T(8,128)(2,1)}), bf16[16,128,256]{2,1,0:T(8,128)(2,1)}) %all-gather.14.cloned.1.call-update) | async-done | bytes 1048592 | tf_op jit(solution)/shard_map/all_gather | solution.py:206
  337.9 2.8 shard_map.72
  345.6 3.9 collective-permute-done.15.b_ref
  349.5 6.6 %collective-permute-done.16.c_ref = f32[2,128,256]{2,1,0:T(8,128)S(1)} collective-permute-done((f32[2,128,256]{2,1,0:T(8,128)S(1)}, f32[2,128,256]{2,1,0:T(8,128)S(1)}, u32[]{:S(2)}, u32[]{:S(2)}) %collective-permute-start.16) | collective-permute-done | bytes 262176 | tf_op jit(solution)/shard_map/ppermute | solution.py:34
  358.6 2.9 collective-permute-done.18.e_ref
  361.7 13.3 %all_to_all.39.in_ref = f32[8,8,128]{2,1,0:T(8,128)S(1)} all-to-all(f32[8,8,128]{2,1,0:T(8,128)S(1)} %get-tuple-element.68), channel_id=1, replica_groups=mesh['x'=4,'yh'=2,'yl'=2,'z'=8,'core'=2] {'x','yh'}, dimensions={0} | all-to-all | bytes 65536 | tf_op jit(solution)/shard_map/all_to_all | solution.py:29
  375.1 18.8 %all_to_all.40.sums_ref = f32[32,8,128]{2,1,0:T(8,128)S(1)} all-to-all(f32[32,8,128]{2,1,0:T(8,128)S(1)} %shard_map.75), channel_id=1, replica_groups=mesh['x'=4,'yh'=2,'yl'=2,'z'=8,'core'=2] {'yl','z','core'}, dimensions={0} | all-to-all | bytes 262144 | tf_op jit(solution)/shard_map/all_to_all | solution.py:29
  (63 shorter events, 52.9 us)
Async XLA Ops:
  7.2 47.1 %copy-start.7 = (s32[256]{0:T(256)S(1)}, s32[256]{0:T(256)}, u32[]{:S(2)}) copy-start(s32[256]{0:T(256)} %param.7) | copy-start | bytes 3076
  8.5 19.1 %all-to-all-start = ((s32[32,1,256]{2,1,0:T(1,128)}), s32[32,1,256]{2,1,0:T(1,128)S(1)}, u32[]{:S(2)}, u32[]{:S(2)}) async-start(s32[32,1,256]{2,1,0:T(1,128)} %broadcast_in_dim.15), calls=%async_computation | async-start | bytes 65536 | tf_op jit(solution)/shard_map/all_to_all | solution.py:29
  19.7 88.1 %all-gather.10.cloned.1.call-start = ((), (), s32[]{:S(2)}) async-start(), calls=%async_computation.7 | async-start | bytes 1572864 | tf_op jit(solution)/shard_map/all_gather | solution.py:206
  27.6 2.8 copy-start
  33.3 8.5 %collective-permute-start = (f32[2,136,256]{2,1,0:T(8,128)S(1)}, f32[2,136,256]{2,1,0:T(8,128)S(1)}, u32[]{:S(2)}, u32[]{:S(2)}) collective-permute-start(f32[2,136,256]{2,1,0:T(8,128)S(1)} %get-tuple-element.38), channel_id=1, source_target_pairs={{0,64},{64,128},{128,192},{192,0},{1,65},{65,129},{129,193},{193,1... | collective-permute-start | bytes 835592 | tf_op jit(solution)/shard_map/ppermute | solution.py:34
  34.5 14.2 %collective-permute-start.1 = (f32[2,136,256]{2,1,0:T(8,128)S(1)}, f32[2,136,256]{2,1,0:T(8,128)S(1)}, u32[]{:S(2)}, u32[]{:S(2)}) collective-permute-start(f32[2,136,256]{2,1,0:T(8,128)S(1)} %get-tuple-element.39), channel_id=1, source_target_pairs={{0,128},{64,192},{128,0},{192,64},{1,129},{65,193},{129,1},{193,65... | collective-permute-start | bytes 835592 | tf_op jit(solution)/shard_map/ppermute | solution.py:34
  37.0 11.8 %collective-permute-start.2 = (f32[2,136,256]{2,1,0:T(8,128)S(1)}, f32[2,136,256]{2,1,0:T(8,128)S(1)}, u32[]{:S(2)}, u32[]{:S(2)}) collective-permute-start(f32[2,136,256]{2,1,0:T(8,128)S(1)} %get-tuple-element.40), channel_id=1, source_target_pairs={{0,192},{64,0},{128,64},{192,128},{1,193},{65,1},{129,65},{193,129... | collective-permute-start | bytes 835592 | tf_op jit(solution)/shard_map/ppermute | solution.py:34
  48.8 5.5 %collective-permute-start.3 = (f32[136,256]{1,0:T(8,128)S(1)}, f32[136,256]{1,0:T(8,128)S(1)}, u32[]{:S(2)}, u32[]{:S(2)}) collective-permute-start(f32[136,256]{1,0:T(8,128)S(1)} %shard_map.60), channel_id=1, source_target_pairs={{0,32},{32,0},{1,33},{33,1},{2,34},{34,2},{3,35},{35,3},{4,36},{36... | collective-permute-start | bytes 417800 | tf_op jit(solution)/shard_map/ppermute | solution.py:34
  76.3 143.0 %all-gather.12.cloned.1.call-start = ((), (), s32[]{:S(2)}) async-start(), calls=%async_computation.8 | async-start | bytes 1572864 | tf_op jit(solution)/shard_map/all_gather | solution.py:206
  107.8 3.2 collective-permute-start.4
  111.0 2.8 copy-start.1
  113.8 1.2 copy-start.4
  117.8 8.8 %collective-permute-start.5 = (f32[2,128,256]{2,1,0:T(8,128)S(1)}, f32[2,128,256]{2,1,0:T(8,128)S(1)}, u32[]{:S(2)}, u32[]{:S(2)}) collective-permute-start(f32[2,128,256]{2,1,0:T(8,128)S(1)} %get-tuple-element.43), channel_id=1, source_target_pairs={{0,64},{64,128},{128,192},{192,0},{1,65},{65,129},{129,193},{193,1... | collective-permute-start | bytes 786440 | tf_op jit(solution)/shard_map/ppermute | solution.py:34
  119.1 14.1 %collective-permute-start.6 = (f32[2,128,256]{2,1,0:T(8,128)S(1)}, f32[2,128,256]{2,1,0:T(8,128)S(1)}, u32[]{:S(2)}, u32[]{:S(2)}) collective-permute-start(f32[2,128,256]{2,1,0:T(8,128)S(1)} %get-tuple-element.44), channel_id=1, source_target_pairs={{0,128},{64,192},{128,0},{192,64},{1,129},{65,193},{129,1},{193,65... | collective-permute-start | bytes 786440 | tf_op jit(solution)/shard_map/ppermute | solution.py:34
  121.5 11.7 %collective-permute-start.7 = (f32[2,128,256]{2,1,0:T(8,128)S(1)}, f32[2,128,256]{2,1,0:T(8,128)S(1)}, u32[]{:S(2)}, u32[]{:S(2)}) collective-permute-start(f32[2,128,256]{2,1,0:T(8,128)S(1)} %get-tuple-element.45), channel_id=1, source_target_pairs={{0,192},{64,0},{128,64},{192,128},{1,193},{65,1},{129,65},{193,129... | collective-permute-start | bytes 786440 | tf_op jit(solution)/shard_map/ppermute | solution.py:34
  133.2 5.4 %collective-permute-start.8 = (f32[128,256]{1,0:T(8,128)S(1)}, f32[128,256]{1,0:T(8,128)S(1)}, u32[]{:S(2)}, u32[]{:S(2)}) collective-permute-start(f32[128,256]{1,0:T(8,128)S(1)} %shard_map.63), channel_id=1, source_target_pairs={{0,32},{32,0},{1,33},{33,1},{2,34},{34,2},{3,35},{35,3},{4,36},{36... | collective-permute-start | bytes 393224 | tf_op jit(solution)/shard_map/ppermute | solution.py:34
  192.7 138.0 %all-gather.14.cloned.1.call-start = ((), (), s32[]{:S(2)}) async-start(), calls=%async_computation.9 | async-start | bytes 1572864 | tf_op jit(solution)/shard_map/all_gather | solution.py:206
  219.3 3.2 collective-permute-start.9
  222.4 2.8 copy-start.2
  225.2 1.2 copy-start.5
  229.3 8.8 %collective-permute-start.10 = (f32[2,128,256]{2,1,0:T(8,128)S(1)}, f32[2,128,256]{2,1,0:T(8,128)S(1)}, u32[]{:S(2)}, u32[]{:S(2)}) collective-permute-start(f32[2,128,256]{2,1,0:T(8,128)S(1)} %get-tuple-element.52), channel_id=1, source_target_pairs={{0,64},{64,128},{128,192},{192,0},{1,65},{65,129},{129,193},{193,1... | collective-permute-start | bytes 786440 | tf_op jit(solution)/shard_map/ppermute | solution.py:34
  230.5 14.1 %collective-permute-start.11 = (f32[2,128,256]{2,1,0:T(8,128)S(1)}, f32[2,128,256]{2,1,0:T(8,128)S(1)}, u32[]{:S(2)}, u32[]{:S(2)}) collective-permute-start(f32[2,128,256]{2,1,0:T(8,128)S(1)} %get-tuple-element.53), channel_id=1, source_target_pairs={{0,128},{64,192},{128,0},{192,64},{1,129},{65,193},{129,1},{193,65... | collective-permute-start | bytes 786440 | tf_op jit(solution)/shard_map/ppermute | solution.py:34
  232.9 11.7 %collective-permute-start.12 = (f32[2,128,256]{2,1,0:T(8,128)S(1)}, f32[2,128,256]{2,1,0:T(8,128)S(1)}, u32[]{:S(2)}, u32[]{:S(2)}) collective-permute-start(f32[2,128,256]{2,1,0:T(8,128)S(1)} %get-tuple-element.54), channel_id=1, source_target_pairs={{0,192},{64,0},{128,64},{192,128},{1,193},{65,1},{129,65},{193,129... | collective-permute-start | bytes 786440 | tf_op jit(solution)/shard_map/ppermute | solution.py:34
  244.7 5.4 %collective-permute-start.13 = (f32[128,256]{1,0:T(8,128)S(1)}, f32[128,256]{1,0:T(8,128)S(1)}, u32[]{:S(2)}, u32[]{:S(2)}) collective-permute-start(f32[128,256]{1,0:T(8,128)S(1)} %shard_map.68), channel_id=1, source_target_pairs={{0,32},{32,0},{1,33},{33,1},{2,34},{34,2},{3,35},{35,3},{4,36},{36... | collective-permute-start | bytes 393224 | tf_op jit(solution)/shard_map/ppermute | solution.py:34
  330.7 3.2 collective-permute-start.14
  333.9 2.8 copy-start.3
  336.7 1.2 copy-start.6
  340.7 8.8 %collective-permute-start.15 = (f32[2,128,256]{2,1,0:T(8,128)S(1)}, f32[2,128,256]{2,1,0:T(8,128)S(1)}, u32[]{:S(2)}, u32[]{:S(2)}) collective-permute-start(f32[2,128,256]{2,1,0:T(8,128)S(1)} %get-tuple-element.63), channel_id=1, source_target_pairs={{0,64},{64,128},{128,192},{192,0},{1,65},{65,129},{129,193},{193,1... | collective-permute-start | bytes 786440 | tf_op jit(solution)/shard_map/ppermute | solution.py:34
  342.0 14.1 %collective-permute-start.16 = (f32[2,128,256]{2,1,0:T(8,128)S(1)}, f32[2,128,256]{2,1,0:T(8,128)S(1)}, u32[]{:S(2)}, u32[]{:S(2)}) collective-permute-start(f32[2,128,256]{2,1,0:T(8,128)S(1)} %get-tuple-element.64), channel_id=1, source_target_pairs={{0,128},{64,192},{128,0},{192,64},{1,129},{65,193},{129,1},{193,65... | collective-permute-start | bytes 786440 | tf_op jit(solution)/shard_map/ppermute | solution.py:34
  344.4 11.7 %collective-permute-start.17 = (f32[2,128,256]{2,1,0:T(8,128)S(1)}, f32[2,128,256]{2,1,0:T(8,128)S(1)}, u32[]{:S(2)}, u32[]{:S(2)}) collective-permute-start(f32[2,128,256]{2,1,0:T(8,128)S(1)} %get-tuple-element.65), channel_id=1, source_target_pairs={{0,192},{64,0},{128,64},{192,128},{1,193},{65,1},{129,65},{193,129... | collective-permute-start | bytes 786440 | tf_op jit(solution)/shard_map/ppermute | solution.py:34
  356.1 5.4 %collective-permute-start.18 = (f32[128,256]{1,0:T(8,128)S(1)}, f32[128,256]{1,0:T(8,128)S(1)}, u32[]{:S(2)}, u32[]{:S(2)}) collective-permute-start(f32[128,256]{1,0:T(8,128)S(1)} %shard_map.73), channel_id=1, source_target_pairs={{0,32},{32,0},{1,33},{33,1},{2,34},{34,2},{3,35},{35,3},{4,36},{36... | collective-permute-start | bytes 393224 | tf_op jit(solution)/shard_map/ppermute | solution.py:34
Sparse Core Ops, SparseCore 0:
  76.4 31.3 all-gather.9
  192.9 26.3 all-gather.11
  304.3 26.3 all-gather.13

commit v2 on v0

v2 whole, which is shorter than its diff:
```python
import functools

import jax
import jax.numpy as jnp
from jax import lax
from jax.experimental import pallas as pl
from jax.experimental.pallas import tpu as pltpu
from jax.sharding import Mesh
from jax.sharding import PartitionSpec as P

CLASSES = 128
ITERS = 3
CHAINS = 1
PART = CLASSES // CHAINS
AXES = ("x", "yh", "yl", "z", "core")
ROW = ("x", "yh")
COL = ("yl", "z", "core")
CHIPS = ("yl", "z")
NEAR = ("x", "yh", "yl", "core")
FAR = ("z",)
F32 = jnp.float32
BF16 = jnp.bfloat16
CHUNK = 8
PARAMS = pltpu.CompilerParams(vmem_limit_bytes=50 * 1024 * 1024)
VMEM = pl.BlockSpec(memory_space=pltpu.VMEM)
SMEM = pl.BlockSpec(memory_space=pltpu.SMEM)
HBM = pl.BlockSpec(memory_space=pltpu.HBM)


def shape(dims, dtype=F32):
    return jax.ShapeDtypeStruct(dims, dtype)


def exchange(blocks, axis):
    return lax.all_to_all(blocks, axis, 0, 0, tiled=True)


def call(kernel, out_shape, *args):
    return pl.pallas_call(
        kernel,
        in_specs=[VMEM] * len(args),
        out_specs=jax.tree.map(lambda _: VMEM, out_shape),
        out_shape=out_shape,
        compiler_params=PARAMS,
    )(*args)


def apply_tiles(kernel, out_shape, source, target, tiles, *panels):
    count = tiles.shape[0]
    return pl.pallas_call(
        kernel,
        in_specs=[SMEM, SMEM, HBM] + [VMEM] * len(panels),
        out_specs=jax.tree.map(lambda _: VMEM, out_shape),
        out_shape=out_shape,
        scratch_shapes=[
            pltpu.VMEM(tiles.shape, tiles.dtype),
            pltpu.SemaphoreType.DMA((count // CHUNK,)),
        ],
        compiler_params=PARAMS,
    )(source, target, tiles, *panels)


def each_tile(tiles_ref, held, arrived, work):
    def chunk(step):
        span = pl.ds(step * CHUNK, CHUNK)
        return pltpu.make_async_copy(tiles_ref.at[span], held.at[span], arrived.at[step])

    steps = held.shape[0] // CHUNK
    for step in range(steps):
        chunk(step).start()
    for step in range(steps):
        chunk(step).wait()
        for at in range(step * CHUNK, (step + 1) * CHUNK):
            work(at, held[at])


def label_kernel(source_ref, target_ref, tiles_ref, label_ref, *rest):
    *parts, degree_ref, held, arrived = rest
    size = held.shape[1]
    classes = lax.broadcasted_iota(jnp.int32, (CLASSES, size), 0)
    for part in parts:
        part[...] = jnp.zeros_like(part)
    degree_ref[...] = jnp.zeros_like(degree_ref)

    def work(at, tile):
        hot = jnp.where(label_ref[source_ref[at]] == classes, F32(1.0), F32(0.0))
        panel = jnp.concatenate([hot, jnp.ones((16, size), F32)], axis=0).astype(BF16)
        product = jnp.dot(panel, tile, preferred_element_type=F32)
        target = target_ref[at]
        for h, part in enumerate(parts):
            part[target] += product[h * PART : (h + 1) * PART]
        degree_ref[target] += product[CLASSES : CLASSES + 1]

    each_tile(tiles_ref, held, arrived, work)


def panel_kernel(source_ref, target_ref, tiles_ref, own_ref, other_ref, out_ref, held, arrived):
    half = own_ref.shape[0]
    out_ref[...] = jnp.zeros_like(out_ref)

    def work(at, tile):
        source = source_ref[at]
        place = lax.rem(source, half)
        panel = jnp.where(source < half, own_ref[place], other_ref[place])
        out_ref[target_ref[at]] += jnp.dot(panel, tile, preferred_element_type=F32)

    each_tile(tiles_ref, held, arrived, work)


def diagonal():
    across = lax.broadcasted_iota(jnp.int32, (PART, PART), 1)
    return lax.broadcasted_iota(jnp.int32, (PART, PART), 0) == across


def to_row(column):
    return jnp.sum(jnp.where(diagonal(), column, F32(0.0)), axis=0, keepdims=True)


def to_column(row):
    return jnp.sum(jnp.where(diagonal(), row, F32(0.0)), axis=1, keepdims=True)


def start_kernel(arrived_ref, label_ref, rhs_ref, panels_ref):
    mixed = jnp.sum(arrived_ref[...], axis=0)
    rhs = jnp.where(label_ref[...] < 0, mixed, F32(0.0))
    rhs_ref[...] = rhs
    panel = rhs.astype(BF16)
    for i in range(panels_ref.shape[0]):
        panels_ref[i] = panel


def image_kernel(
    first, arrived_ref, label_ref, degree_ref, direction_ref, residual_ref, image_ref, sums_ref
):
    mixed = jnp.sum(arrived_ref[...], axis=0)
    degree = degree_ref[...]
    direction = direction_ref[...]
    residual = residual_ref[...]
    image = jnp.where(label_ref[...] < 0, degree * direction - mixed, direction)
    image_ref[...] = image
    terms = (direction * image, residual * (residual if first else image), image * image)
    sums = [to_row(jnp.sum(term, axis=1, keepdims=True)) for term in terms]
    sums = jnp.concatenate(sums, axis=1)
    sums_ref[...] = jnp.broadcast_to(sums[None], sums_ref.shape)


def relay_kernel(in_ref, out_ref):
    out_ref[...] = jnp.broadcast_to(jnp.sum(in_ref[...], axis=0)[None], out_ref.shape)


def step_kernel(
    first, sums_ref, norm_ref, solution_ref, residual_ref, direction_ref, image_ref,
    solution_out, residual_out, direction_out, panels_out, norm_out,
):
    sums = jnp.sum(sums_ref[...], axis=0)
    bending, crossed, energy = (sums[:, PART * i : PART * (i + 1)] for i in range(3))
    if first:
        norm, crossed = crossed, bending
    else:
        norm = norm_ref[...]
    alpha = norm / bending
    norm_next = norm - 2.0 * alpha * crossed + alpha * alpha * energy
    norm_out[...] = norm_next
    beta = to_column(norm_next / norm)
    alpha = to_column(alpha)
    direction = direction_ref[...]
    step = alpha * direction
    solution_out[...] = step if first else solution_ref[...] + step
    residual = residual_ref[...] - alpha * image_ref[...]
    residual_out[...] = residual
    direction = residual + beta * direction
    direction_out[...] = direction
    panel = direction.astype(BF16)
    for i in range(panels_out.shape[0]):
        panels_out[i] = panel


def last_kernel(*refs):
    *ins, scores_out, residual_out = refs
    scores, residuals = [], []
    for h in range(CHAINS):
        sums_ref, norm_ref, solution_ref, residual_ref, direction_ref, image_ref = ins[6 * h : 6 * h + 6]
        sums = jnp.sum(sums_ref[...], axis=0)
        alpha = to_column(norm_ref[...] / sums[:, :PART])
        scores.append(8.0 * CLASSES * (solution_ref[...] + alpha * direction_ref[...]))
        residuals.append(residual_ref[...] - alpha * image_ref[...])
    scores_out[...] = jnp.concatenate(scores, axis=0).T
    residual_out[...] = jnp.concatenate(residuals, axis=0).T


def reduce_by_permutes(parts):
    x = lax.axis_index("x")
    parts = parts.reshape(4, 2, *parts.shape[1:])
    total = parts[x]
    for by in range(1, 4):
        moves = [(i, (i + by) % 4) for i in range(4)]
        total = total + lax.ppermute(parts[(x + by) % 4], "x", moves)
    y = lax.axis_index("yh")
    return total[y] + lax.ppermute(total[1 - y], "yh", [(0, 1), (1, 0)])


def shards(tiles, tile_row, tile_col, label_class):
    size = tiles.shape[1]
    near = lax.axis_size(NEAR)
    far = lax.axis_size(FAR)
    rows = lax.axis_size(ROW)
    cols = lax.axis_size(COL)
    chips = lax.axis_size(CHIPS)
    local = tile_row % cols
    mine = local % 2 == lax.axis_index("core")
    source = local // 2 + jnp.where(mine, 0, chips)
    target = tile_col // cols
    label = label_class.reshape(1, size)
    labels = exchange(jnp.broadcast_to(label[None], (cols, 1, size)), COL)
    out_part = shape((rows, PART, size))
    *sent, degree = apply_tiles(
        label_kernel, (*[out_part] * CHAINS, shape((rows, 1, size))), local, target, tiles, labels
    )
    field = shape((PART, size))
    panels_out = shape((chips, PART, size), BF16)
    norm_out = shape((1, PART))
    arrived = [exchange(s, ROW) for s in sent]
    degree = reduce_by_permutes(degree)
    chains = []
    for h in range(CHAINS):
        residual, panels = call(start_kernel, (field, panels_out), arrived[h], label)
        chains.append((residual, residual, residual, panels, jnp.zeros((1, PART), F32)))
    for iteration in range(ITERS):
        states = []
        for solution, residual, direction, panels, norm in chains:
            own = exchange(panels, CHIPS)
            other = lax.ppermute(own, "core", [(0, 1), (1, 0)])
            partial = apply_tiles(panel_kernel, out_part, source, target, tiles, own, other)
            image, sums = call(
                functools.partial(image_kernel, iteration == 0),
                (field, shape((near, 1, 3 * PART))),
                exchange(partial, ROW), label, degree, direction, residual,
            )
            sums = call(relay_kernel, shape((far, 1, 3 * PART)), exchange(sums, NEAR))
            states.append((exchange(sums, FAR), norm, solution, residual, direction, image))
        if iteration + 1 < ITERS:
            step = functools.partial(step_kernel, iteration == 0)
            chains = [call(step, (field, field, field, panels_out, norm_out), *s) for s in states]
    out = shape((size, CLASSES))
    return call(last_kernel, (out, out), *[a for s in states for a in s])


def solution(mesh):
    torus = Mesh(mesh.devices.reshape(4, 2, 2, 8, 2), AXES)
    return jax.shard_map(
        shards,
        mesh=torus,
        in_specs=(P(AXES, None, None), P(AXES), P(AXES), P(AXES)),
        out_specs=(P(AXES, None), P(AXES, None)),
        check_vma=False,
    )
```

time: 579 us -> 290 us (0.50)
  blocking collectives: 328 us -> 210 us
  waiting for transfers between devices: 93.8 us -> 27.7 us
  other arithmetic: 53.7 us -> 0.7 us
  local copies, waits for them, and re-layouts: 42 us -> 1.39 us
  matrix products: 30.1 us -> 0 us
  Pallas kernels: 0 us -> 18.8 us
  starting transfers between devices: 15.9 us -> 30.3 us
  between operations: 14.2 us -> 0.75 us
    psum x15 -> x0, blocking collectives: 131 us -> none  [over_axes(): return functools.reduce(lax.psum, axes, array)]
    reduce_scatter x1 -> x0, waiting for transfers between devices: 79.5 us -> none  [side_by_side(): lax.psum_scatter(both, axis, scatter_dimension=dim, tiled=True)]
    scatter-add x5 -> x0, other arithmetic: 42.8 us -> none  [the longest x4 42 us: tile_apply(): return jax.ops.segment_sum(products, target, num_segments=segment_count)]
    dot_general x4 -> x0, matrix products: 30.1 us -> none  [tile_apply(): jnp.einsum(einsum_form, tiles, gathered, preferred_element_type=jnp.float32)]
    dot_general x4 -> x0, local copies, waits for them, and re-layouts: 26.2 us -> none  [tile_apply(): jnp.einsum(einsum_form, tiles, gathered, preferred_element_type=jnp.float32)]
    ppermute x0 -> x7, waiting for transfers between devices: none -> 20.5 us  [the longest x3 11.3 us: reduce_by_permutes(): total = total + lax.ppermute(parts[(x + by) % 4], 'x', moves)]
    pallas_call x0 -> x14, Pallas kernels: none -> 18.8 us  [the longest x4 16.6 us: apply_tiles(): pl.pallas_call(kernel, in_specs=[SMEM, SMEM, HBM] + [VMEM] * len(panels),...]
    ppermute x0 -> x7, starting transfers between devices: none -> 15.2 us  [the longest x3 9.05 us: shards(): other = lax.ppermute(own, 'core', [(0, 1), (1, 0)])]
  transfers between devices with their start and end apart: 3 -> 9, of which waited for: 3 -> 8; matrix products, arithmetic and copies ran while one was open for 1% -> 0% of each run, Pallas kernels for 0% -> 0%
where the time goes in v2:
time: 290 us; the launch traced here: 289 us
  blocking collectives  210 us (72%)
  starting transfers between devices  30.3 us (10%)
  waiting for transfers between devices  27.7 us (10%)
  Pallas kernels  18.8 us (6%)
    all_to_all x12, blocking collectives, exchange(): return lax.all_to_all(blocks, axis, 0, 0, tiled=True)  210 us
    pallas_call x4, Pallas kernels, apply_tiles(): pl.pallas_call(kernel, in_specs=[SMEM, SMEM, HBM] + [VMEM] * len(panels),...  16.6 us
    all_to_all x2, starting transfers between devices, exchange(): return lax.all_to_all(blocks, axis, 0, 0, tiled=True)  15.2 us
    ppermute x3, waiting for transfers between devices, reduce_by_permutes(): total = total + lax.ppermute(parts[(x + by) % 4], 'x', moves)  11.3 us
    ppermute x3, starting transfers between devices, shards(): other = lax.ppermute(own, 'core', [(0, 1), (1, 0)])  9.05 us
    all_to_all x2, waiting for transfers between devices, exchange(): return lax.all_to_all(blocks, axis, 0, 0, tiled=True)  7.23 us
    ppermute x3, waiting for transfers between devices, shards(): other = lax.ppermute(own, 'core', [(0, 1), (1, 0)])  6.86 us
  transfers between devices with their start and end apart: 9, of which 8 were waited for; matrix products, arithmetic and copies ran while one was open for 0% of the time, Pallas kernels for 0%

profile of v2, /device:TPU:1, one launch (start us, length us, event | category | flops | bytes accessed | tf_op | source)
XLA Modules:
  0.0 289.3 jit_solution(518894814596596673)
XLA Ops:
  2.0 11.1 %all-to-all-start = ((s32[32,1,256]{2,1,0:T(1,128)}), s32[32,1,256]{2,1,0:T(1,128)S(1)}, u32[]{:S(2)}, u32[]{:S(2)}) async-start(s32[32,1,256]{2,1,0:T(1,128)} %broadcast_in_dim.15), calls=%async_computation | async-start | bytes 65536 | tf_op jit(solution)/shard_map/all_to_all | solution.py:35
  13.9 7.2 %all-to-all-done.label_ref = s32[32,1,256]{2,1,0:T(1,128)S(1)} async-done(((s32[32,1,256]{2,1,0:T(1,128)}), s32[32,1,256]{2,1,0:T(1,128)S(1)}, u32[]{:S(2)}, u32[]{:S(2)}) %all-to-all-start) | async-done | bytes 32800 | tf_op jit(solution)/shard_map/all_to_all | solution.py:35
  21.1 3.8 %shard_map.59 = (f32[8,128,256]{2,1,0:T(8,128)S(1)}, f32[8,1,256]{2,1,0:T(1,128)S(1)}) custom-call(s32[48]{0:T(128)S(1)} %get-tuple-element.43.source_ref, s32[48]{0:T(128)S(1)} %get-tuple-element.47.target_ref, bf16[48,256,256]{2,1,0:T(8,128)(2,1)} %tiles_ref.7, s32[32,1,256]{2,1,0:T(1,128)S(1)} %all-to-all-done.label_ref), custom_call_target="tpu_custom_call" | custom-call | tf_op jit(solution)/shard_map/pallas_call | solution.py:50
  24.9 21.2 %all_to_all.70.arrived_ref = f32[8,128,256]{2,1,0:T(8,128)S(1)} all-to-all(f32[8,128,256]{2,1,0:T(8,128)S(1)} %get-tuple-element.22), channel_id=1, replica_groups=mesh['x'=4,'yh'=2,'yl'=2,'z'=8,'core'=2] {'x','yh'}, dimensions={0} | all-to-all | bytes 2097152 | tf_op jit(solution)/shard_map/all_to_all | solution.py:35
  46.2 26.3 %all_to_all.71.own_ref = bf16[16,128,256]{2,1,0:T(8,128)(2,1)S(1)} all-to-all(bf16[16,128,256]{2,1,0:T(8,128)(2,1)S(1)} %get-tuple-element.23), channel_id=1, replica_groups=mesh['x'=4,'yh'=2,'yl'=2,'z'=8,'core'=2] {'yl','z'}, dimensions={0} | all-to-all | bytes 2097152 | tf_op jit(solution)/shard_map/all_to_all | solution.py:35
  72.5 3.7 %collective-permute-start = (bf16[16,128,256]{2,1,0:T(8,128)(2,1)S(1)}, bf16[16,128,256]{2,1,0:T(8,128)(2,1)S(1)}, u32[]{:S(2)}, u32[]{:S(2)}) collective-permute-start(bf16[16,128,256]{2,1,0:T(8,128)(2,1)S(1)} %all_to_all.71.own_ref), channel_id=1, source_target_pairs={{0,1},{1,0},{2,3},{3,2},{4,5},{5,4},{6,7},{7,6},{8,9},{9,8},{10,11... | collective-permute-start | bytes 3145736 | tf_op jit(solution)/shard_map/ppermute | solution.py:232
  76.2 2.3 collective-permute-done.other_ref
  78.4 4.9 %shard_map.61 = f32[8,128,256]{2,1,0:T(8,128)} custom-call(s32[48]{0:T(128)S(1)} %get-tuple-element.42.source_ref, s32[48]{0:T(128)S(1)} %get-tuple-element.47.target_ref, bf16[48,256,256]{2,1,0:T(8,128)(2,1)} %tiles_ref.7, bf16[16,128,256]{2,1,0:T(8,128)(2,1)S(1)} %all_to_all.71.own_ref, bf16[16,128,256]{2,1,0:T(8,128)(2,1)S(1)} %collective-permute-done.other_ref), custom_call_target="tpu_custom_call" | custom-call | tf_op jit(solution)/shard_map/pallas_call | solution.py:50
  83.4 4.0 %all-to-all-start.3 = ((f32[8,128,256]{2,1,0:T(8,128)}), f32[8,128,256]{2,1,0:T(8,128)S(1)}, u32[]{:S(2)}, u32[]{:S(2)}) async-start(f32[8,128,256]{2,1,0:T(8,128)} %shard_map.61), calls=%async_computation.3 | async-start | bytes 2097152 | tf_op jit(solution)/shard_map/all_to_all | solution.py:35
  87.4 1.5 collective-permute-start.1
  90.2 1.7 collective-permute-start.2
  91.8 7.1 %collective-permute-done.1 = f32[2,1,256]{2,1,0:T(1,128)S(1)} collective-permute-done((f32[2,1,256]{2,1,0:T(1,128)S(1)}, f32[2,1,256]{2,1,0:T(1,128)S(1)}, u32[]{:S(2)}, u32[]{:S(2)}) %collective-permute-start.1) | collective-permute-done | bytes 2080 | tf_op jit(solution)/shard_map/ppermute | solution.py:197
  98.9 1.6 collective-permute-done.3
  100.5 2.6 collective-permute-done.2
  103.2 1.7 collective-permute-start.4
  104.9 2.3 collective-permute-done.4
  107.4 14.4 %all_to_all.72.in_ref = f32[32,1,384]{2,1,0:T(1,128)S(1)} all-to-all(f32[32,1,384]{2,1,0:T(1,128)S(1)} %get-tuple-element.26), channel_id=1, replica_groups=mesh['x'=4,'yh'=2,'yl'=2,'z'=8,'core'=2] {'x','yh','yl','core'}, dimensions={0} | all-to-all | bytes 98304 | tf_op jit(solution)/shard_map/all_to_all | solution.py:35
  121.9 10.3 %all_to_all.73.sums_ref = f32[8,1,384]{2,1,0:T(1,128)S(1)} all-to-all(f32[8,1,384]{2,1,0:T(1,128)S(1)} %shard_map.63), channel_id=1, replica_groups=mesh['x'=4,'yh'=2,'yl'=2,'z'=8,'core'=2] {'z'}, dimensions={0} | all-to-all | bytes 24576 | tf_op jit(solution)/shard_map/all_to_all | solution.py:35
  132.4 27.2 %all_to_all.74.own_ref = bf16[16,128,256]{2,1,0:T(8,128)(2,1)S(1)} all-to-all(bf16[16,128,256]{2,1,0:T(8,128)(2,1)S(1)} %get-tuple-element.28), channel_id=1, replica_groups=mesh['x'=4,'yh'=2,'yl'=2,'z'=8,'core'=2] {'yl','z'}, dimensions={0} | all-to-all | bytes 2097152 | tf_op jit(solution)/shard_map/all_to_all | solution.py:35
  159.6 2.7 collective-permute-start.5
  162.3 2.3 collective-permute-done.5.other_ref
  164.6 3.9 %shard_map.65 = f32[8,128,256]{2,1,0:T(8,128)S(1)} custom-call(s32[48]{0:T(128)S(1)} %get-tuple-element.42.source_ref, s32[48]{0:T(128)S(1)} %get-tuple-element.47.target_ref, bf16[48,256,256]{2,1,0:T(8,128)(2,1)} %tiles_ref.7, bf16[16,128,256]{2,1,0:T(8,128)(2,1)S(1)} %all_to_all.74.own_ref, bf16[16,128,256]{2,1,0:T(8,128)(2,1)S(1)} %collective-permute-done.5.other_ref), custom_call_target="tpu_custom_call" | custom-call | tf_op jit(solution)/shard_map/pallas_call | solution.py:50
  168.5 18.4 %all_to_all.75.arrived_ref = f32[8,128,256]{2,1,0:T(8,128)S(1)} all-to-all(f32[8,128,256]{2,1,0:T(8,128)S(1)} %shard_map.65), channel_id=1, replica_groups=mesh['x'=4,'yh'=2,'yl'=2,'z'=8,'core'=2] {'x','yh'}, dimensions={0} | all-to-all | bytes 2097152 | tf_op jit(solution)/shard_map/all_to_all | solution.py:35
  187.1 12.6 %all_to_all.76.in_ref = f32[32,1,384]{2,1,0:T(1,128)S(1)} all-to-all(f32[32,1,384]{2,1,0:T(1,128)S(1)} %get-tuple-element.31), channel_id=1, replica_groups=mesh['x'=4,'yh'=2,'yl'=2,'z'=8,'core'=2] {'x','yh','yl','core'}, dimensions={0} | all-to-all | bytes 98304 | tf_op jit(solution)/shard_map/all_to_all | solution.py:35
  199.8 10.6 %all_to_all.77.sums_ref = f32[8,1,384]{2,1,0:T(1,128)S(1)} all-to-all(f32[8,1,384]{2,1,0:T(1,128)S(1)} %shard_map.67), channel_id=1, replica_groups=mesh['x'=4,'yh'=2,'yl'=2,'z'=8,'core'=2] {'z'}, dimensions={0} | all-to-all | bytes 24576 | tf_op jit(solution)/shard_map/all_to_all | solution.py:35
  210.6 27.2 %all_to_all.78.own_ref = bf16[16,128,256]{2,1,0:T(8,128)(2,1)S(1)} all-to-all(bf16[16,128,256]{2,1,0:T(8,128)(2,1)S(1)} %get-tuple-element.35), channel_id=1, replica_groups=mesh['x'=4,'yh'=2,'yl'=2,'z'=8,'core'=2] {'yl','z'}, dimensions={0} | all-to-all | bytes 2097152 | tf_op jit(solution)/shard_map/all_to_all | solution.py:35
  237.8 2.7 collective-permute-start.6
  240.5 2.3 collective-permute-done.6.other_ref
  242.8 3.9 %shard_map.69 = f32[8,128,256]{2,1,0:T(8,128)S(1)} custom-call(s32[48]{0:T(128)S(1)} %get-tuple-element.42.source_ref, s32[48]{0:T(128)S(1)} %get-tuple-element.47.target_ref, bf16[48,256,256]{2,1,0:T(8,128)(2,1)} %tiles_ref.7, bf16[16,128,256]{2,1,0:T(8,128)(2,1)S(1)} %all_to_all.78.own_ref, bf16[16,128,256]{2,1,0:T(8,128)(2,1)S(1)} %collective-permute-done.6.other_ref), custom_call_target="tpu_custom_call" | custom-call | tf_op jit(solution)/shard_map/pallas_call | solution.py:50
  246.8 18.2 %all_to_all.79.arrived_ref = f32[8,128,256]{2,1,0:T(8,128)S(1)} all-to-all(f32[8,128,256]{2,1,0:T(8,128)S(1)} %shard_map.69), channel_id=1, replica_groups=mesh['x'=4,'yh'=2,'yl'=2,'z'=8,'core'=2] {'x','yh'}, dimensions={0} | all-to-all | bytes 2097152 | tf_op jit(solution)/shard_map/all_to_all | solution.py:35
  265.2 12.6 %all_to_all.80.in_ref = f32[32,1,384]{2,1,0:T(1,128)S(1)} all-to-all(f32[32,1,384]{2,1,0:T(1,128)S(1)} %get-tuple-element.38), channel_id=1, replica_groups=mesh['x'=4,'yh'=2,'yl'=2,'z'=8,'core'=2] {'x','yh','yl','core'}, dimensions={0} | all-to-all | bytes 98304 | tf_op jit(solution)/shard_map/all_to_all | solution.py:35
  277.8 10.6 %all_to_all.81.refs_0_ = f32[8,1,384]{2,1,0:T(1,128)S(1)} all-to-all(f32[8,1,384]{2,1,0:T(1,128)S(1)} %shard_map.71), channel_id=1, replica_groups=mesh['x'=4,'yh'=2,'yl'=2,'z'=8,'core'=2] {'z'}, dimensions={0} | all-to-all | bytes 24576 | tf_op jit(solution)/shard_map/all_to_all | solution.py:35
  (21 shorter events, 5.5 us)
Async XLA Ops:
  0.6 45.5 %copy-start = (s32[256]{0:T(256)S(1)}, s32[256]{0:T(256)}, u32[]{:S(2)}) copy-start(s32[256]{0:T(256)} %param.7) | copy-start | bytes 3076
  2.0 19.1 %all-to-all-start = ((s32[32,1,256]{2,1,0:T(1,128)}), s32[32,1,256]{2,1,0:T(1,128)S(1)}, u32[]{:S(2)}, u32[]{:S(2)}) async-start(s32[32,1,256]{2,1,0:T(1,128)} %broadcast_in_dim.15), calls=%async_computation | async-start | bytes 65536 | tf_op jit(solution)/shard_map/all_to_all | solution.py:35
  72.5 5.9 %collective-permute-start = (bf16[16,128,256]{2,1,0:T(8,128)(2,1)S(1)}, bf16[16,128,256]{2,1,0:T(8,128)(2,1)S(1)}, u32[]{:S(2)}, u32[]{:S(2)}) collective-permute-start(bf16[16,128,256]{2,1,0:T(8,128)(2,1)S(1)} %all_to_all.71.own_ref), channel_id=1, source_target_pairs={{0,1},{1,0},{2,3},{3,2},{4,5},{5,4},{6,7},{7,6},{8,9},{9,8},{10,11... | collective-permute-start | bytes 3145736 | tf_op jit(solution)/shard_map/ppermute | solution.py:232
  83.4 23.9 %all-to-all-start.3 = ((f32[8,128,256]{2,1,0:T(8,128)}), f32[8,128,256]{2,1,0:T(8,128)S(1)}, u32[]{:S(2)}, u32[]{:S(2)}) async-start(f32[8,128,256]{2,1,0:T(8,128)} %shard_map.61), calls=%async_computation.3 | async-start | bytes 2097152 | tf_op jit(solution)/shard_map/all_to_all | solution.py:35
  87.4 11.5 %collective-permute-start.1 = (f32[2,1,256]{2,1,0:T(1,128)S(1)}, f32[2,1,256]{2,1,0:T(1,128)S(1)}, u32[]{:S(2)}, u32[]{:S(2)}) collective-permute-start(f32[2,1,256]{2,1,0:T(1,128)S(1)} %get-tuple-element.44), channel_id=1, source_target_pairs={{0,64},{64,128},{128,192},{192,0},{1,65},{65,129},{129,193},{193,1... | collective-permute-start | bytes 6152 | tf_op jit(solution)/shard_map/ppermute | solution.py:197
  88.9 11.7 %collective-permute-start.3 = (f32[2,1,256]{2,1,0:T(1,128)S(1)}, f32[2,1,256]{2,1,0:T(1,128)S(1)}, u32[]{:S(2)}, u32[]{:S(2)}) collective-permute-start(f32[2,1,256]{2,1,0:T(1,128)S(1)} %get-tuple-element.45), channel_id=1, source_target_pairs={{0,192},{64,0},{128,64},{192,128},{1,193},{65,1},{129,65},{193,129... | collective-permute-start | bytes 6152 | tf_op jit(solution)/shard_map/ppermute | solution.py:197
  90.2 13.0 %collective-permute-start.2 = (f32[2,1,256]{2,1,0:T(1,128)S(1)}, f32[2,1,256]{2,1,0:T(1,128)S(1)}, u32[]{:S(2)}, u32[]{:S(2)}) collective-permute-start(f32[2,1,256]{2,1,0:T(1,128)S(1)} %get-tuple-element.46), channel_id=1, source_target_pairs={{0,128},{64,192},{128,0},{192,64},{1,129},{65,193},{129,1},{193,65... | collective-permute-start | bytes 6152 | tf_op jit(solution)/shard_map/ppermute | solution.py:197
  103.2 4.0 %collective-permute-start.4 = (f32[1,256]{1,0:T(1,128)S(1)}, f32[1,256]{1,0:T(1,128)S(1)}, u32[]{:S(2)}, u32[]{:S(2)}) collective-permute-start(f32[1,256]{1,0:T(1,128)S(1)} %fusion.4), channel_id=1, source_target_pairs={{0,32},{32,0},{1,33},{33,1},{2,34},{34,2},{3,35},{35,3},{4,36},{36... | collective-permute-start | bytes 3080 | tf_op jit(solution)/shard_map/ppermute | solution.py:199
  159.6 5.0 %collective-permute-start.5 = (bf16[16,128,256]{2,1,0:T(8,128)(2,1)S(1)}, bf16[16,128,256]{2,1,0:T(8,128)(2,1)S(1)}, u32[]{:S(2)}, u32[]{:S(2)}) collective-permute-start(bf16[16,128,256]{2,1,0:T(8,128)(2,1)S(1)} %all_to_all.74.own_ref), channel_id=1, source_target_pairs={{0,1},{1,0},{2,3},{3,2},{4,5},{5,4},{6,7},{7,6},{8,9},{9,8},{10,11... | collective-permute-start | bytes 3145736 | tf_op jit(solution)/shard_map/ppermute | solution.py:232
  237.8 5.0 %collective-permute-start.6 = (bf16[16,128,256]{2,1,0:T(8,128)(2,1)S(1)}, bf16[16,128,256]{2,1,0:T(8,128)(2,1)S(1)}, u32[]{:S(2)}, u32[]{:S(2)}) collective-permute-start(bf16[16,128,256]{2,1,0:T(8,128)(2,1)S(1)} %all_to_all.78.own_ref), channel_id=1, source_target_pairs={{0,1},{1,0},{2,3},{3,2},{4,5},{5,4},{6,7},{7,6},{8,9},{9,8},{10,11... | collective-permute-start | bytes 3145736 | tf_op jit(solution)/shard_map/ppermute | solution.py:232

commit v3 on v2

v3 whole, which is shorter than its diff:
```python
import jax
import jax.numpy as jnp
from jax import lax
from jax.experimental import pallas as pl
from jax.experimental.pallas import tpu as pltpu
from jax.sharding import Mesh
from jax.sharding import PartitionSpec as P

CLASSES = 128
SHIFT = 4.0
TINY = 1e-30
AXES = ("x", "yh", "yl", "z", "core")
ROW = ("x", "yh")
COL = ("yl", "z", "core")
CHIPS = ("yl", "z")
NEAR = ("x", "yh", "yl", "core")
FAR = ("z",)
F32 = jnp.float32
BF16 = jnp.bfloat16
CHUNK = 8
PARAMS = pltpu.CompilerParams(vmem_limit_bytes=50 * 1024 * 1024)
VMEM = pl.BlockSpec(memory_space=pltpu.VMEM)
SMEM = pl.BlockSpec(memory_space=pltpu.SMEM)
HBM = pl.BlockSpec(memory_space=pltpu.HBM)


def shape(dims, dtype=F32):
    return jax.ShapeDtypeStruct(dims, dtype)


def exchange(blocks, axis):
    return lax.all_to_all(blocks, axis, 0, 0, tiled=True)


def call(kernel, out_shape, *args):
    return pl.pallas_call(
        kernel,
        in_specs=[VMEM] * len(args),
        out_specs=jax.tree.map(lambda _: VMEM, out_shape),
        out_shape=out_shape,
        compiler_params=PARAMS,
    )(*args)


def apply_tiles(kernel, out_shape, scalars, tiles, *panels):
    count = tiles.shape[0]
    return pl.pallas_call(
        kernel,
        in_specs=[SMEM] * len(scalars) + [HBM] + [VMEM] * len(panels),
        out_specs=jax.tree.map(lambda _: VMEM, out_shape),
        out_shape=out_shape,
        scratch_shapes=[
            pltpu.VMEM(tiles.shape, tiles.dtype),
            pltpu.SemaphoreType.DMA((count // CHUNK,)),
        ],
        compiler_params=PARAMS,
    )(*scalars, tiles, *panels)


def each_tile(tiles_ref, held, arrived, prepare, work):
    def chunk(step):
        span = pl.ds(step * CHUNK, CHUNK)
        return pltpu.make_async_copy(tiles_ref.at[span], held.at[span], arrived.at[step])

    steps = held.shape[0] // CHUNK
    for step in range(steps):
        chunk(step).start()
    prepare()
    for step in range(steps):
        chunk(step).wait()
        for at in range(step * CHUNK, (step + 1) * CHUNK):
            work(at, held[at])


def label_kernel(
    source_ref, target_ref, tiles_ref, label_ref, out_ref, degree_ref, count_ref, held, arrived
):
    size = held.shape[1]
    classes = lax.broadcasted_iota(jnp.int32, (CLASSES, size), 0)

    def prepare():
        out_ref[...] = jnp.zeros_like(out_ref)
        degree_ref[...] = jnp.zeros_like(degree_ref)
        count = jnp.sum(jnp.where(label_ref[...] < 0, F32(1.0), F32(0.0)), axis=0)
        count_ref[...] = jnp.broadcast_to(jnp.sum(count, axis=1, keepdims=True), count_ref.shape)

    def work(at, tile):
        hot = jnp.where(label_ref[source_ref[at]] == classes, F32(1.0), F32(0.0))
        panel = jnp.concatenate([hot, jnp.ones((16, size), F32)], axis=0).astype(BF16)
        product = jnp.dot(panel, tile, preferred_element_type=F32)
        target = target_ref[at]
        out_ref[target] += product[:CLASSES]
        degree_ref[target] += product[CLASSES : CLASSES + 1]

    each_tile(tiles_ref, held, arrived, prepare, work)


def total_of(panels_ref):
    total = panels_ref[0].astype(F32)
    for i in range(1, panels_ref.shape[0]):
        total = total + panels_ref[i].astype(F32)
    return jnp.sum(jnp.sum(total, axis=0, keepdims=True), axis=1, keepdims=True)


def multiply_panels(source_ref, target_ref, tiles_ref, own_ref, other_ref, out_ref, held, arrived, prepare):
    half = own_ref.shape[0]

    def work(at, tile):
        source = source_ref[at]
        place = lax.rem(source, half)
        panel = jnp.where(source < half, own_ref[place], other_ref[place])
        out_ref[target_ref[at]] += jnp.dot(panel, tile, preferred_element_type=F32)

    each_tile(tiles_ref, held, arrived, prepare, work)


def first_panel_kernel(
    source_ref, target_ref, tiles_ref, own_ref, other_ref, count_ref, out_ref, shift_ref, held, arrived
):
    def prepare():
        out_ref[...] = jnp.zeros_like(out_ref)
        total = total_of(own_ref) + total_of(other_ref)
        shift_ref[...] = SHIFT * total / jnp.maximum(count_ref[...], 1.0)

    multiply_panels(
        source_ref, target_ref, tiles_ref, own_ref, other_ref, out_ref, held, arrived, prepare
    )


def shifted_panel_kernel(
    source_ref, target_ref, tiles_ref, own_ref, other_ref, last_ref, shift_ref, out_ref, held, arrived
):
    def prepare():
        for i in range(out_ref.shape[0]):
            out_ref[i] = shift_ref[:, :1] * last_ref[i]

    multiply_panels(
        source_ref, target_ref, tiles_ref, own_ref, other_ref, out_ref, held, arrived, prepare
    )


def panel_kernel(source_ref, target_ref, tiles_ref, own_ref, other_ref, out_ref, held, arrived):
    def prepare():
        out_ref[...] = jnp.zeros_like(out_ref)

    multiply_panels(
        source_ref, target_ref, tiles_ref, own_ref, other_ref, out_ref, held, arrived, prepare
    )


def diagonal():
    across = lax.broadcasted_iota(jnp.int32, (CLASSES, CLASSES), 1)
    return lax.broadcasted_iota(jnp.int32, (CLASSES, CLASSES), 0) == across


def to_row(column):
    return jnp.sum(jnp.where(diagonal(), column, F32(0.0)), axis=0, keepdims=True)


def to_column(row):
    return jnp.sum(jnp.where(diagonal(), row, F32(0.0)), axis=1, keepdims=True)


def to_all(value, copies_ref):
    for i in range(copies_ref.shape[0]):
        copies_ref[i] = value


def start_kernel(arrived_ref, label_ref, rhs_ref, panels_ref):
    mixed = jnp.sum(arrived_ref[...], axis=0)
    rhs = jnp.where(label_ref[...] < 0, mixed, F32(0.0))
    rhs_ref[...] = rhs
    to_all(rhs.astype(BF16), panels_ref)


def applied(arrived_ref, label_ref, degree_ref, field):
    mixed = jnp.sum(arrived_ref[...], axis=0)
    return jnp.where(label_ref[...] < 0, degree_ref[...] * field - mixed, field)


def inner_products(pairs, sums_ref, more=()):
    sums = [to_row(jnp.sum(a * b, axis=1, keepdims=True)) for a, b in pairs]
    to_all(jnp.concatenate([*sums, *more], axis=1), sums_ref)


def image_kernel(arrived_ref, label_ref, degree_ref, shift_ref, rhs_ref, image_ref, panels_ref):
    rhs = rhs_ref[...]
    image = applied(arrived_ref, label_ref, degree_ref, rhs)
    image_ref[...] = image
    to_all((image - shift_ref[:, :1] * rhs).astype(BF16), panels_ref)


TIMES = (0, 1, 2, 2, 3, 4)


def second_kernel(arrived_ref, label_ref, degree_ref, rhs_ref, image_ref, second_ref, sums_ref):
    rhs, image = rhs_ref[...], image_ref[...]
    second = applied(arrived_ref, label_ref, degree_ref, image)
    second_ref[...] = second
    degree = degree_ref[...]
    scale = jnp.sum(degree, axis=1, keepdims=True) / degree.shape[1]
    scale = jnp.maximum(scale, F32(TINY))
    image = image / scale
    second = second / scale / scale
    pairs = ((rhs, rhs), (rhs, image), (image, image), (rhs, second), (image, second), (second, second))
    inner_products(pairs, sums_ref, [jnp.broadcast_to(scale, (1, CLASSES))])


def pooled(sums):
    part = [sums[:, :, CLASSES * i : CLASSES * (i + 1)] for i in range(7)]
    scale = jnp.max(part[6], axis=0)
    powers = [jnp.ones_like(part[6]), part[6] / scale[None]]
    for _ in range(3):
        powers.append(powers[-1] * powers[1])
    return [jnp.sum(p * powers[t], axis=0) for p, t in zip(part, TIMES)] + [scale]


def pool_kernel(in_ref, out_ref):
    to_all(jnp.concatenate(pooled(in_ref[...]), axis=1), out_ref)


def relay_kernel(in_ref, out_ref):
    to_all(jnp.sum(in_ref[...], axis=0), out_ref)


def two_steps_kernel(
    sums_ref, rhs_ref, image_ref, second_ref,
    solution_out, residual_out, direction_out, panels_out, norm_out,
):
    bb, bp, pp, bs, ps, ss, scale = pooled(sums_ref[...])
    alpha = bb / bp
    norm = bb - 2.0 * alpha * bp + alpha * alpha * pp
    beta = norm / bb
    more = 1.0 + beta
    square = alpha * alpha
    bending = more * more * bp - alpha * more * (bs + pp) + square * ps
    crossed = more * bp - alpha * bs - alpha * more * pp + square * ps
    energy = more * more * pp - 2.0 * alpha * more * ps + square * ss
    alpha_next = norm / bending
    norm_next = norm - 2.0 * alpha_next * crossed + alpha_next * alpha_next * energy
    norm_out[...] = norm_next
    beta_next = to_column(norm_next / norm)
    alpha, alpha_next = to_column(alpha / scale), to_column(alpha_next / scale)
    beta = to_column(beta)
    rhs, image = rhs_ref[...], image_ref[...]
    residual = rhs - alpha * image
    direction = residual + beta * rhs
    solution_out[...] = alpha * rhs + alpha_next * direction
    image_next = (1.0 + beta) * image - alpha * second_ref[...]
    residual = residual - alpha_next * image_next
    residual_out[...] = residual
    direction = residual + beta_next * direction
    direction_out[...] = direction
    to_all(direction.astype(BF16), panels_out)


def third_kernel(arrived_ref, label_ref, degree_ref, direction_ref, image_ref, sums_ref):
    direction = direction_ref[...]
    image = applied(arrived_ref, label_ref, degree_ref, direction)
    image_ref[...] = image
    inner_products(((direction, image),), sums_ref)


def last_kernel(
    sums_ref, norm_ref, solution_ref, residual_ref, direction_ref, image_ref,
    scores_out, residual_out,
):
    alpha = to_column(norm_ref[...] / jnp.sum(sums_ref[...], axis=0))
    total = solution_ref[...] + alpha * direction_ref[...]
    scores_out[...] = (8.0 * CLASSES * total).T
    residual_out[...] = (residual_ref[...] - alpha * image_ref[...]).T


def reduce_by_permutes(parts):
    x = lax.axis_index("x")
    parts = parts.reshape(4, 2, *parts.shape[1:])
    total = parts[x]
    for by in range(1, 4):
        moves = [(i, (i + by) % 4) for i in range(4)]
        total = total + lax.ppermute(parts[(x + by) % 4], "x", moves)
    y = lax.axis_index("yh")
    return total[y] + lax.ppermute(total[1 - y], "yh", [(0, 1), (1, 0)])


def shards(tiles, tile_row, tile_col, label_class):
    size = tiles.shape[1]
    near = lax.axis_size(NEAR)
    far = lax.axis_size(FAR)
    rows = lax.axis_size(ROW)
    cols = lax.axis_size(COL)
    chips = lax.axis_size(CHIPS)
    local = tile_row % cols
    mine = local % 2 == lax.axis_index("core")
    source = local // 2 + jnp.where(mine, 0, chips)
    target = tile_col // cols
    label = label_class.reshape(1, size)
    partial_out = shape((rows, CLASSES, size))
    field = shape((CLASSES, size))
    panels_out = shape((chips, CLASSES, size), BF16)
    row_out = shape((1, CLASSES))

    def gather(panels):
        own = exchange(panels, CHIPS)
        return own, lax.ppermute(own, "core", [(0, 1), (1, 0)])

    def everywhere(kernel, sums):
        sums = exchange(sums, NEAR)
        return exchange(call(kernel, shape((far, *sums.shape[1:])), sums), FAR)

    labels = exchange(jnp.broadcast_to(label[None], (cols, 1, size)), COL)
    partial, share, count = apply_tiles(
        label_kernel, (partial_out, shape((rows, 1, size)), row_out), (local, target), tiles, labels
    )
    rhs, panels = call(start_kernel, (field, panels_out), exchange(partial, ROW), label)
    degree = reduce_by_permutes(share)
    partial, shift = apply_tiles(
        first_panel_kernel, (partial_out, row_out), (source, target), tiles, *gather(panels), count
    )
    image, panels = call(
        image_kernel, (field, panels_out), exchange(partial, ROW), label, degree, shift, rhs
    )
    partial = apply_tiles(
        shifted_panel_kernel, partial_out, (source, target), tiles, *gather(panels), partial, shift
    )
    second, sums = call(
        second_kernel, (field, shape((near, 1, 7 * CLASSES))),
        exchange(partial, ROW), label, degree, rhs, image,
    )
    solution, residual, direction, panels, norm = call(
        two_steps_kernel, (field, field, field, panels_out, row_out),
        everywhere(pool_kernel, sums), rhs, image, second,
    )
    partial = apply_tiles(panel_kernel, partial_out, (source, target), tiles, *gather(panels))
    image, sums = call(
        third_kernel, (field, shape((near, 1, CLASSES))),
        exchange(partial, ROW), label, degree, direction,
    )
    out = shape((size, CLASSES))
    return call(
        last_kernel, (out, out), everywhere(relay_kernel, sums), norm, solution, residual, direction, image
    )


def solution(mesh):
    torus = Mesh(mesh.devices.reshape(4, 2, 2, 8, 2), AXES)
    return jax.shard_map(
        shards,
        mesh=torus,
        in_specs=(P(AXES, None, None), P(AXES), P(AXES), P(AXES)),
        out_specs=(P(AXES, None), P(AXES, None)),
        check_vma=False,
    )
```

time: 290 us -> 269 us (0.928)
  blocking collectives: 210 us -> 187 us
    all_to_all x12 -> x10, blocking collectives: 210 us -> 187 us  [exchange(): return lax.all_to_all(blocks, axis, 0, 0, tiled=True)]
where the time goes in v3:
time: 269 us
  blocking collectives  187 us (70%)
  starting transfers between devices  31.5 us (12%)
  waiting for transfers between devices  27.7 us (10%)
  Pallas kernels  19.2 us (7%)
    all_to_all x10, blocking collectives, exchange(): return lax.all_to_all(blocks, axis, 0, 0, tiled=True)  187 us
    pallas_call x4, Pallas kernels, apply_tiles(): pl.pallas_call(kernel, in_specs=[SMEM] * len(scalars) + [HBM] + [VMEM] *...  17.2 us
    all_to_all x2, starting transfers between devices, exchange(): return lax.all_to_all(blocks, axis, 0, 0, tiled=True)  15.1 us
    ppermute x3, waiting for transfers between devices, reduce_by_permutes(): total = total + lax.ppermute(parts[(x + by) % 4], 'x', moves)  11.3 us
    ppermute x3, starting transfers between devices, gather(): return (own, lax.ppermute(own, 'core', [(0, 1), (1, 0)]))  10.3 us
    all_to_all x2, waiting for transfers between devices, exchange(): return lax.all_to_all(blocks, axis, 0, 0, tiled=True)  7.23 us
    ppermute x3, waiting for transfers between devices, gather(): return (own, lax.ppermute(own, 'core', [(0, 1), (1, 0)]))  6.86 us
  transfers between devices with their start and end apart: 9, of which 8 were waited for; matrix products, arithmetic and copies ran while one was open for 0% of the time, Pallas kernels for 0%

profile of v3, /device:TPU:1, one launch (start us, length us, event | category | flops | bytes accessed | tf_op | source)
XLA Modules:
  0.0 268.6 jit_solution(15412631896759552114)
XLA Ops:
  0.6 1.4 broadcast_in_dim.12
  2.0 11.1 %all-to-all-start = ((s32[32,1,256]{2,1,0:T(1,128)}), s32[32,1,256]{2,1,0:T(1,128)S(1)}, u32[]{:S(2)}, u32[]{:S(2)}) async-start(s32[32,1,256]{2,1,0:T(1,128)} %broadcast_in_dim.12), calls=%async_computation | async-start | bytes 65536 | tf_op jit(solution)/shard_map/all_to_all | solution.py:32
  13.9 7.2 %all-to-all-done.label_ref = s32[32,1,256]{2,1,0:T(1,128)S(1)} async-done(((s32[32,1,256]{2,1,0:T(1,128)}), s32[32,1,256]{2,1,0:T(1,128)S(1)}, u32[]{:S(2)}, u32[]{:S(2)}) %all-to-all-start) | async-done | bytes 32800 | tf_op jit(solution)/shard_map/all_to_all | solution.py:32
  21.1 3.8 %shard_map.59 = (f32[8,128,256]{2,1,0:T(8,128)S(1)}, f32[8,1,256]{2,1,0:T(1,128)S(1)}, f32[1,128]{1,0:T(1,128)S(1)}) custom-call(s32[48]{0:T(128)S(1)} %get-tuple-element.39.source_ref, s32[48]{0:T(128)S(1)} %get-tuple-element.43.target_ref, bf16[48,256,256]{2,1,0:T(8,128)(2,1)} %tiles_ref.7, s32[32,1,256]{2,1,0:T(1,128)S(1)} %all-to-all-done.label_ref), custom_call_target="tpu_custom_call" | custom-call | tf_op jit(solution)/shard_map/pallas_call | solution.py:47
  24.9 21.1 %all_to_all.60.arrived_ref = f32[8,128,256]{2,1,0:T(8,128)S(1)} all-to-all(f32[8,128,256]{2,1,0:T(8,128)S(1)} %get-tuple-element.20), channel_id=1, replica_groups=mesh['x'=4,'yh'=2,'yl'=2,'z'=8,'core'=2] {'x','yh'}, dimensions={0} | all-to-all | bytes 2097152 | tf_op jit(solution)/shard_map/all_to_all | solution.py:32
  46.2 26.3 %all_to_all.61.own_ref = bf16[16,128,256]{2,1,0:T(8,128)(2,1)S(1)} all-to-all(bf16[16,128,256]{2,1,0:T(8,128)(2,1)S(1)} %get-tuple-element.21), channel_id=1, replica_groups=mesh['x'=4,'yh'=2,'yl'=2,'z'=8,'core'=2] {'yl','z'}, dimensions={0} | all-to-all | bytes 2097152 | tf_op jit(solution)/shard_map/all_to_all | solution.py:32
  72.5 3.7 %collective-permute-start = (bf16[16,128,256]{2,1,0:T(8,128)(2,1)S(1)}, bf16[16,128,256]{2,1,0:T(8,128)(2,1)S(1)}, u32[]{:S(2)}, u32[]{:S(2)}) collective-permute-start(bf16[16,128,256]{2,1,0:T(8,128)(2,1)S(1)} %all_to_all.61.own_ref), channel_id=1, source_target_pairs={{0,1},{1,0},{2,3},{3,2},{4,5},{5,4},{6,7},{7,6},{8,9},{9,8},{10,11... | collective-permute-start | bytes 3145736 | tf_op jit(solution)/shard_map/ppermute | solution.py:304
  76.3 2.3 collective-permute-done.other_ref
  78.5 4.8 %shard_map.61 = (f32[8,128,256]{2,1,0:T(8,128)}, f32[1,128]{1,0:T(1,128)S(1)}) custom-call(s32[48]{0:T(128)S(1)} %get-tuple-element.38.source_ref, s32[48]{0:T(128)S(1)} %get-tuple-element.43.target_ref, bf16[48,256,256]{2,1,0:T(8,128)(2,1)} %tiles_ref.7, bf16[16,128,256]{2,1,0:T(8,128)(2,1)S(1)} %all_to_all.61.own_ref, ...), custom_call_target="tpu_custom_call" | custom-call | tf_op jit(solution)/shard_map/pallas_call | solution.py:47
  83.4 3.9 %all-to-all-start.3 = ((f32[8,128,256]{2,1,0:T(8,128)}), f32[8,128,256]{2,1,0:T(8,128)S(1)}, u32[]{:S(2)}, u32[]{:S(2)}) async-start(f32[8,128,256]{2,1,0:T(8,128)} %get-tuple-element.23.last_ref), calls=%async_computation.3 | async-start | bytes 2097152 | tf_op jit(solution)/shard_map/all_to_all | solution.py:32
  87.4 1.5 collective-permute-start.1
  88.8 1.3 collective-permute-start.3
  90.1 1.7 collective-permute-start.2
  91.8 7.1 %collective-permute-done.1 = f32[2,1,256]{2,1,0:T(1,128)S(1)} collective-permute-done((f32[2,1,256]{2,1,0:T(1,128)S(1)}, f32[2,1,256]{2,1,0:T(1,128)S(1)}, u32[]{:S(2)}, u32[]{:S(2)}) %collective-permute-start.1) | collective-permute-done | bytes 2080 | tf_op jit(solution)/shard_map/ppermute | solution.py:280
  98.9 1.6 collective-permute-done.3
  100.5 2.6 collective-permute-done.2
  103.2 1.7 collective-permute-start.4
  104.9 2.3 collective-permute-done.4
  107.3 28.3 %all_to_all.62.own_ref = bf16[16,128,256]{2,1,0:T(8,128)(2,1)S(1)} all-to-all(bf16[16,128,256]{2,1,0:T(8,128)(2,1)S(1)} %get-tuple-element.27), channel_id=1, replica_groups=mesh['x'=4,'yh'=2,'yl'=2,'z'=8,'core'=2] {'yl','z'}, dimensions={0} | all-to-all | bytes 2097152 | tf_op jit(solution)/shard_map/all_to_all | solution.py:32
  135.6 3.8 %collective-permute-start.5 = (bf16[16,128,256]{2,1,0:T(8,128)(2,1)S(1)}, bf16[16,128,256]{2,1,0:T(8,128)(2,1)S(1)}, u32[]{:S(2)}, u32[]{:S(2)}) collective-permute-start(bf16[16,128,256]{2,1,0:T(8,128)(2,1)S(1)} %all_to_all.62.own_ref), channel_id=1, source_target_pairs={{0,1},{1,0},{2,3},{3,2},{4,5},{5,4},{6,7},{7,6},{8,9},{9,8},{10,11... | collective-permute-start | bytes 3145736 | tf_op jit(solution)/shard_map/ppermute | solution.py:304
  139.4 2.3 collective-permute-done.5.other_ref
  141.7 4.5 %shard_map.63 = f32[8,128,256]{2,1,0:T(8,128)S(1)} custom-call(s32[48]{0:T(128)S(1)} %get-tuple-element.38.source_ref, s32[48]{0:T(128)S(1)} %get-tuple-element.43.target_ref, bf16[48,256,256]{2,1,0:T(8,128)(2,1)} %tiles_ref.7, bf16[16,128,256]{2,1,0:T(8,128)(2,1)S(1)} %all_to_all.62.own_ref, bf16[16,128,256]{2,1,0:T(8,128)(2,1)S(1)} %collective-permute-done.5.other_ref, ...), custom_call_target="tpu_custom_call" | custom-call | tf_op jit(solution)/shard_map/pallas_call | solution.py:47
  146.2 19.6 %all_to_all.63.arrived_ref = f32[8,128,256]{2,1,0:T(8,128)S(1)} all-to-all(f32[8,128,256]{2,1,0:T(8,128)S(1)} %shard_map.63), channel_id=1, replica_groups=mesh['x'=4,'yh'=2,'yl'=2,'z'=8,'core'=2] {'x','yh'}, dimensions={0} | all-to-all | bytes 2097152 | tf_op jit(solution)/shard_map/all_to_all | solution.py:32
  166.1 13.0 %all_to_all.64.in_ref = f32[32,1,896]{2,1,0:T(1,128)S(1)} all-to-all(f32[32,1,896]{2,1,0:T(1,128)S(1)} %get-tuple-element.29), channel_id=1, replica_groups=mesh['x'=4,'yh'=2,'yl'=2,'z'=8,'core'=2] {'x','yh','yl','core'}, dimensions={0} | all-to-all | bytes 229376 | tf_op jit(solution)/shard_map/all_to_all | solution.py:32
  179.3 10.8 %all_to_all.65.sums_ref = f32[8,1,896]{2,1,0:T(1,128)S(1)} all-to-all(f32[8,1,896]{2,1,0:T(1,128)S(1)} %shard_map.65), channel_id=1, replica_groups=mesh['x'=4,'yh'=2,'yl'=2,'z'=8,'core'=2] {'z'}, dimensions={0} | all-to-all | bytes 57344 | tf_op jit(solution)/shard_map/all_to_all | solution.py:32
  190.4 27.2 %all_to_all.66.own_ref = bf16[16,128,256]{2,1,0:T(8,128)(2,1)S(1)} all-to-all(bf16[16,128,256]{2,1,0:T(8,128)(2,1)S(1)} %get-tuple-element.31), channel_id=1, replica_groups=mesh['x'=4,'yh'=2,'yl'=2,'z'=8,'core'=2] {'yl','z'}, dimensions={0} | all-to-all | bytes 2097152 | tf_op jit(solution)/shard_map/all_to_all | solution.py:32
  217.5 2.7 %collective-permute-start.6 = (bf16[16,128,256]{2,1,0:T(8,128)(2,1)S(1)}, bf16[16,128,256]{2,1,0:T(8,128)(2,1)S(1)}, u32[]{:S(2)}, u32[]{:S(2)}) collective-permute-start(bf16[16,128,256]{2,1,0:T(8,128)(2,1)S(1)} %all_to_all.66.own_ref), channel_id=1, source_target_pairs={{0,1},{1,0},{2,3},{3,2},{4,5},{5,4},{6,7},{7,6},{8,9},{9,8},{10,11... | collective-permute-start | bytes 3145736 | tf_op jit(solution)/shard_map/ppermute | solution.py:304
  220.3 2.3 collective-permute-done.6.other_ref
  222.6 3.9 %shard_map.67 = f32[8,128,256]{2,1,0:T(8,128)S(1)} custom-call(s32[48]{0:T(128)S(1)} %get-tuple-element.38.source_ref, s32[48]{0:T(128)S(1)} %get-tuple-element.43.target_ref, bf16[48,256,256]{2,1,0:T(8,128)(2,1)} %tiles_ref.7, bf16[16,128,256]{2,1,0:T(8,128)(2,1)S(1)} %all_to_all.66.own_ref, bf16[16,128,256]{2,1,0:T(8,128)(2,1)S(1)} %collective-permute-done.6.other_ref), custom_call_target="tpu_custom_call" | custom-call | tf_op jit(solution)/shard_map/pallas_call | solution.py:47
  226.5 18.1 %all_to_all.67.arrived_ref = f32[8,128,256]{2,1,0:T(8,128)S(1)} all-to-all(f32[8,128,256]{2,1,0:T(8,128)S(1)} %shard_map.67), channel_id=1, replica_groups=mesh['x'=4,'yh'=2,'yl'=2,'z'=8,'core'=2] {'x','yh'}, dimensions={0} | all-to-all | bytes 2097152 | tf_op jit(solution)/shard_map/all_to_all | solution.py:32
  244.8 12.4 %all_to_all.68.in_ref = f32[32,1,128]{2,1,0:T(1,128)S(1)} all-to-all(f32[32,1,128]{2,1,0:T(1,128)S(1)} %get-tuple-element.33), channel_id=1, replica_groups=mesh['x'=4,'yh'=2,'yl'=2,'z'=8,'core'=2] {'x','yh','yl','core'}, dimensions={0} | all-to-all | bytes 32768 | tf_op jit(solution)/shard_map/all_to_all | solution.py:32
  257.2 10.5 %all_to_all.69.sums_ref = f32[8,1,128]{2,1,0:T(1,128)S(1)} all-to-all(f32[8,1,128]{2,1,0:T(1,128)S(1)} %shard_map.69), channel_id=1, replica_groups=mesh['x'=4,'yh'=2,'yl'=2,'z'=8,'core'=2] {'z'}, dimensions={0} | all-to-all | bytes 8192 | tf_op jit(solution)/shard_map/all_to_all | solution.py:32
  (16 shorter events, 2.8 us)
Async XLA Ops:
  0.6 45.5 %copy-start = (s32[256]{0:T(256)S(1)}, s32[256]{0:T(256)}, u32[]{:S(2)}) copy-start(s32[256]{0:T(256)} %param.7) | copy-start | bytes 3076
  2.0 19.1 %all-to-all-start = ((s32[32,1,256]{2,1,0:T(1,128)}), s32[32,1,256]{2,1,0:T(1,128)S(1)}, u32[]{:S(2)}, u32[]{:S(2)}) async-start(s32[32,1,256]{2,1,0:T(1,128)} %broadcast_in_dim.12), calls=%async_computation | async-start | bytes 65536 | tf_op jit(solution)/shard_map/all_to_all | solution.py:32
  72.5 6.0 %collective-permute-start = (bf16[16,128,256]{2,1,0:T(8,128)(2,1)S(1)}, bf16[16,128,256]{2,1,0:T(8,128)(2,1)S(1)}, u32[]{:S(2)}, u32[]{:S(2)}) collective-permute-start(bf16[16,128,256]{2,1,0:T(8,128)(2,1)S(1)} %all_to_all.61.own_ref), channel_id=1, source_target_pairs={{0,1},{1,0},{2,3},{3,2},{4,5},{5,4},{6,7},{7,6},{8,9},{9,8},{10,11... | collective-permute-start | bytes 3145736 | tf_op jit(solution)/shard_map/ppermute | solution.py:304
  83.4 23.8 %all-to-all-start.3 = ((f32[8,128,256]{2,1,0:T(8,128)}), f32[8,128,256]{2,1,0:T(8,128)S(1)}, u32[]{:S(2)}, u32[]{:S(2)}) async-start(f32[8,128,256]{2,1,0:T(8,128)} %get-tuple-element.23.last_ref), calls=%async_computation.3 | async-start | bytes 2097152 | tf_op jit(solution)/shard_map/all_to_all | solution.py:32
  87.4 11.5 %collective-permute-start.1 = (f32[2,1,256]{2,1,0:T(1,128)S(1)}, f32[2,1,256]{2,1,0:T(1,128)S(1)}, u32[]{:S(2)}, u32[]{:S(2)}) collective-permute-start(f32[2,1,256]{2,1,0:T(1,128)S(1)} %get-tuple-element.40), channel_id=1, source_target_pairs={{0,64},{64,128},{128,192},{192,0},{1,65},{65,129},{129,193},{193,1... | collective-permute-start | bytes 6152 | tf_op jit(solution)/shard_map/ppermute | solution.py:280
  88.8 11.7 %collective-permute-start.3 = (f32[2,1,256]{2,1,0:T(1,128)S(1)}, f32[2,1,256]{2,1,0:T(1,128)S(1)}, u32[]{:S(2)}, u32[]{:S(2)}) collective-permute-start(f32[2,1,256]{2,1,0:T(1,128)S(1)} %get-tuple-element.41), channel_id=1, source_target_pairs={{0,192},{64,0},{128,64},{192,128},{1,193},{65,1},{129,65},{193,129... | collective-permute-start | bytes 6152 | tf_op jit(solution)/shard_map/ppermute | solution.py:280
  90.1 13.0 %collective-permute-start.2 = (f32[2,1,256]{2,1,0:T(1,128)S(1)}, f32[2,1,256]{2,1,0:T(1,128)S(1)}, u32[]{:S(2)}, u32[]{:S(2)}) collective-permute-start(f32[2,1,256]{2,1,0:T(1,128)S(1)} %get-tuple-element.42), channel_id=1, source_target_pairs={{0,128},{64,192},{128,0},{192,64},{1,129},{65,193},{129,1},{193,65... | collective-permute-start | bytes 6152 | tf_op jit(solution)/shard_map/ppermute | solution.py:280
  103.2 4.0 %collective-permute-start.4 = (f32[1,256]{1,0:T(1,128)S(1)}, f32[1,256]{1,0:T(1,128)S(1)}, u32[]{:S(2)}, u32[]{:S(2)}) collective-permute-start(f32[1,256]{1,0:T(1,128)S(1)} %fusion.4), channel_id=1, source_target_pairs={{0,32},{32,0},{1,33},{33,1},{2,34},{34,2},{3,35},{35,3},{4,36},{36... | collective-permute-start | bytes 3080 | tf_op jit(solution)/shard_map/ppermute | solution.py:282
  135.6 6.1 %collective-permute-start.5 = (bf16[16,128,256]{2,1,0:T(8,128)(2,1)S(1)}, bf16[16,128,256]{2,1,0:T(8,128)(2,1)S(1)}, u32[]{:S(2)}, u32[]{:S(2)}) collective-permute-start(bf16[16,128,256]{2,1,0:T(8,128)(2,1)S(1)} %all_to_all.62.own_ref), channel_id=1, source_target_pairs={{0,1},{1,0},{2,3},{3,2},{4,5},{5,4},{6,7},{7,6},{8,9},{9,8},{10,11... | collective-permute-start | bytes 3145736 | tf_op jit(solution)/shard_map/ppermute | solution.py:304
  217.5 5.0 %collective-permute-start.6 = (bf16[16,128,256]{2,1,0:T(8,128)(2,1)S(1)}, bf16[16,128,256]{2,1,0:T(8,128)(2,1)S(1)}, u32[]{:S(2)}, u32[]{:S(2)}) collective-permute-start(bf16[16,128,256]{2,1,0:T(8,128)(2,1)S(1)} %all_to_all.66.own_ref), channel_id=1, source_target_pairs={{0,1},{1,0},{2,3},{3,2},{4,5},{5,4},{6,7},{7,6},{8,9},{9,8},{10,11... | collective-permute-start | bytes 3145736 | tf_op jit(solution)/shard_map/ppermute | solution.py:304

commit v4 on v3

--- a/solution.py
+++ b/solution.py
@@ -17,7 +17,7 @@
 FAR = ("z",)
 F32 = jnp.float32
 BF16 = jnp.bfloat16
-CHUNK = 8
+CHUNK = 16
 PARAMS = pltpu.CompilerParams(vmem_limit_bytes=50 * 1024 * 1024)
 VMEM = pl.BlockSpec(memory_space=pltpu.VMEM)
 SMEM = pl.BlockSpec(memory_space=pltpu.SMEM)
@@ -217,10 +217,6 @@
 
 def pool_kernel(in_ref, out_ref):
     to_all(jnp.concatenate(pooled(in_ref[...]), axis=1), out_ref)
-
-
-def relay_kernel(in_ref, out_ref):
-    to_all(jnp.sum(in_ref[...], axis=0), out_ref)
 
 
 def two_steps_kernel(
@@ -271,6 +267,21 @@
     residual_out[...] = (residual_ref[...] - alpha * image_ref[...]).T
 
 
+def after_kernel(own_ref, degree_ref, own_out, degree_out):
+    degree_out[...] = degree_ref[...]
+
+
+def after(own, degree):
+    return pl.pallas_call(
+        after_kernel,
+        in_specs=[pl.BlockSpec(memory_space=pl.ANY), VMEM],
+        out_specs=[pl.BlockSpec(memory_space=pl.ANY), VMEM],
+        out_shape=[shape(own.shape, own.dtype), shape(degree.shape)],
+        input_output_aliases={0: 0},
+        compiler_params=PARAMS,
+    )(own, degree)
+
+
 def reduce_by_permutes(parts):
     x = lax.axis_index("x")
     parts = parts.reshape(4, 2, *parts.shape[1:])
@@ -299,22 +310,25 @@
     panels_out = shape((chips, CLASSES, size), BF16)
     row_out = shape((1, CLASSES))
 
+    def other_core(own):
+        return lax.ppermute(own, "core", [(0, 1), (1, 0)])
+
     def gather(panels):
         own = exchange(panels, CHIPS)
-        return own, lax.ppermute(own, "core", [(0, 1), (1, 0)])
-
-    def everywhere(kernel, sums):
+        return own, other_core(own)
+
+    def everywhere(sums):
         sums = exchange(sums, NEAR)
-        return exchange(call(kernel, shape((far, *sums.shape[1:])), sums), FAR)
+        return exchange(call(pool_kernel, shape((far, *sums.shape[1:])), sums), FAR)
 
     labels = exchange(jnp.broadcast_to(label[None], (cols, 1, size)), COL)
     partial, share, count = apply_tiles(
         label_kernel, (partial_out, shape((rows, 1, size)), row_out), (local, target), tiles, labels
     )
     rhs, panels = call(start_kernel, (field, panels_out), exchange(partial, ROW), label)
-    degree = reduce_by_permutes(share)
+    own, degree = after(exchange(panels, CHIPS), reduce_by_permutes(share))
     partial, shift = apply_tiles(
-        first_panel_kernel, (partial_out, row_out), (source, target), tiles, *gather(panels), count
+        first_panel_kernel, (partial_out, row_out), (source, target), tiles, own, other_core(own), count
     )
     image, panels = call(
         image_kernel, (field, panels_out), exchange(partial, ROW), label, degree, shift, rhs
@@ -328,16 +342,16 @@
     )
     solution, residual, direction, panels, norm = call(
         two_steps_kernel, (field, field, field, panels_out, row_out),
-        everywhere(pool_kernel, sums), rhs, image, second,
+        everywhere(sums), rhs, image, second,
     )
     partial = apply_tiles(panel_kernel, partial_out, (source, target), tiles, *gather(panels))
     image, sums = call(
-        third_kernel, (field, shape((near, 1, CLASSES))),
+        third_kernel, (field, shape((near * far, 1, CLASSES))),
         exchange(partial, ROW), label, degree, direction,
     )
     out = shape((size, CLASSES))
     return call(
-        last_kernel, (out, out), everywhere(relay_kernel, sums), norm, solution, residual, direction, image
+        last_kernel, (out, out), exchange(sums, AXES), norm, solution, residual, direction, image
     )
 
 

time: 269 us -> 264 us (0.981)
  blocking collectives: 187 us -> 178 us
  waiting for transfers between devices: 27.7 us -> 31.7 us
    all_to_all x2, waiting for transfers between devices: 7.23 us -> 18.6 us  [exchange(): return lax.all_to_all(blocks, axis, 0, 0, tiled=True)]
    all_to_all x10 -> x9, blocking collectives: 187 us -> 178 us  [exchange(): return lax.all_to_all(blocks, axis, 0, 0, tiled=True)]
    ppermute x3, waiting for transfers between devices: 11.3 us -> 3.61 us  [reduce_by_permutes(): total = total + lax.ppermute(parts[(x + by) % 4], 'x', moves)]
where the time goes in v4:
time: 264 us
  blocking collectives  178 us (67%)
  waiting for transfers between devices  31.7 us (12%)
  starting transfers between devices  31.2 us (12%)
  Pallas kernels  19.9 us (8%)
    all_to_all x9, blocking collectives, exchange(): return lax.all_to_all(blocks, axis, 0, 0, tiled=True)  178 us
    all_to_all x2, waiting for transfers between devices, exchange(): return lax.all_to_all(blocks, axis, 0, 0, tiled=True)  18.6 us
    pallas_call x4, Pallas kernels, apply_tiles(): pl.pallas_call(kernel, in_specs=[SMEM] * len(scalars) + [HBM] + [VMEM] *...  16.6 us
    all_to_all x2, starting transfers between devices, exchange(): return lax.all_to_all(blocks, axis, 0, 0, tiled=True)  14.8 us
    ppermute x3, starting transfers between devices, other_core(): return lax.ppermute(own, 'core', [(0, 1), (1, 0)])  11.6 us
    ppermute x3, waiting for transfers between devices, other_core(): return lax.ppermute(own, 'core', [(0, 1), (1, 0)])  6.86 us
  transfers between devices with their start and end apart: 9, of which 8 were waited for; matrix products, arithmetic and copies ran while one was open for 0% of the time, Pallas kernels for 0%

profile of v4, /device:TPU:1, one launch (start us, length us, event | category | flops | bytes accessed | tf_op | source)
XLA Modules:
  0.0 263.5 jit_solution(16165694010567260985)
XLA Ops:
  0.6 1.4 broadcast_in_dim.12
  2.0 11.1 %all-to-all-start = ((s32[32,1,256]{2,1,0:T(1,128)}), s32[32,1,256]{2,1,0:T(1,128)S(1)}, u32[]{:S(2)}, u32[]{:S(2)}) async-start(s32[32,1,256]{2,1,0:T(1,128)} %broadcast_in_dim.12), calls=%async_computation | async-start | bytes 65536 | tf_op jit(solution)/shard_map/all_to_all | solution.py:32
  13.2 0.7 fusion.5
  13.9 7.2 %all-to-all-done.label_ref = s32[32,1,256]{2,1,0:T(1,128)S(1)} async-done(((s32[32,1,256]{2,1,0:T(1,128)}), s32[32,1,256]{2,1,0:T(1,128)S(1)}, u32[]{:S(2)}, u32[]{:S(2)}) %all-to-all-start) | async-done | bytes 32800 | tf_op jit(solution)/shard_map/all_to_all | solution.py:32
  21.1 4.0 %shard_map.59 = (f32[8,128,256]{2,1,0:T(8,128)S(1)}, f32[8,1,256]{2,1,0:T(1,128)S(1)}, f32[1,128]{1,0:T(1,128)S(1)}) custom-call(s32[48]{0:T(128)S(1)} %get-tuple-element.43.source_ref, s32[48]{0:T(128)S(1)} %get-tuple-element.47.target_ref, bf16[48,256,256]{2,1,0:T(8,128)(2,1)} %tiles_ref.7, s32[32,1,256]{2,1,0:T(1,128)S(1)} %all-to-all-done.label_ref), custom_call_target="tpu_custom_call" | custom-call | tf_op jit(solution)/shard_map/pallas_call | solution.py:47
  25.0 21.2 %all_to_all.55.arrived_ref = f32[8,128,256]{2,1,0:T(8,128)S(1)} all-to-all(f32[8,128,256]{2,1,0:T(8,128)S(1)} %get-tuple-element.22), channel_id=1, replica_groups=mesh['x'=4,'yh'=2,'yl'=2,'z'=8,'core'=2] {'x','yh'}, dimensions={0} | all-to-all | bytes 2097152 | tf_op jit(solution)/shard_map/all_to_all | solution.py:32
  46.2 1.1 shard_map.60
  47.3 3.7 %all-to-all-start.2 = ((bf16[16,128,256]{2,1,0:T(8,128)(2,1)}), bf16[16,128,256]{2,1,0:T(8,128)(2,1)S(1)}, u32[]{:S(2)}, u32[]{:S(2)}) async-start(bf16[16,128,256]{2,1,0:T(8,128)(2,1)} %get-tuple-element.23), calls=%async_computation.2 | async-start | bytes 2097152 | tf_op jit(solution)/shard_map/all_to_all | solution.py:32
  51.2 2.7 %collective-permute-start.2 = (f32[2,1,256]{2,1,0:T(1,128)S(1)}, f32[2,1,256]{2,1,0:T(1,128)S(1)}, u32[]{:S(2)}, u32[]{:S(2)}) collective-permute-start(f32[2,1,256]{2,1,0:T(1,128)S(1)} %get-tuple-element.45), channel_id=1, source_target_pairs={{0,192},{64,0},{128,64},{192,128},{1,193},{65,1},{129,65},{193,129... | collective-permute-start | bytes 6152 | tf_op jit(solution)/shard_map/ppermute | solution.py:291
  54.1 0.6 collective-permute-done
  54.8 3.0 %collective-permute-done.1 = f32[2,1,256]{2,1,0:T(1,128)S(1)} collective-permute-done((f32[2,1,256]{2,1,0:T(1,128)S(1)}, f32[2,1,256]{2,1,0:T(1,128)S(1)}, u32[]{:S(2)}, u32[]{:S(2)}) %collective-permute-start.1) | collective-permute-done | bytes 2080 | tf_op jit(solution)/shard_map/ppermute | solution.py:291
  57.8 1.7 collective-permute-start.3
  59.5 2.6 collective-permute-done.3
  62.1 11.4 %all-to-all-done.2.own_ref = bf16[16,128,256]{2,1,0:T(8,128)(2,1)S(1)} async-done(((bf16[16,128,256]{2,1,0:T(8,128)(2,1)}), bf16[16,128,256]{2,1,0:T(8,128)(2,1)S(1)}, u32[]{:S(2)}, u32[]{:S(2)}) %all-to-all-start.2) | async-done | bytes 1048608 | tf_op jit(solution)/shard_map/all_to_all | solution.py:32
  73.5 5.4 %collective-permute-start.4 = (bf16[16,128,256]{2,1,0:T(8,128)(2,1)S(1)}, bf16[16,128,256]{2,1,0:T(8,128)(2,1)S(1)}, u32[]{:S(2)}, u32[]{:S(2)}) collective-permute-start(bf16[16,128,256]{2,1,0:T(8,128)(2,1)S(1)} %get-tuple-element.25.own_ref), channel_id=1, source_target_pairs={{0,1},{1,0},{2,3},{3,2},{4,5},{5,4},{6,7},{7,6},{8,9},{9,8},{10,11... | collective-permute-start | bytes 3145736 | tf_op jit(solution)/shard_map/ppermute | solution.py:314
  79.0 2.3 collective-permute-done.4.other_ref
  81.2 4.0 %shard_map.62 = (f32[8,128,256]{2,1,0:T(8,128)S(1)}, f32[1,128]{1,0:T(1,128)S(1)}) custom-call(s32[48]{0:T(128)S(1)} %get-tuple-element.42.source_ref, s32[48]{0:T(128)S(1)} %get-tuple-element.47.target_ref, bf16[48,256,256]{2,1,0:T(8,128)(2,1)} %tiles_ref.7, bf16[16,128,256]{2,1,0:T(8,128)(2,1)S(1)} %get-tuple-element.25.own_ref, ...), custom_call_target="tpu_custom_call" | custom-call | tf_op jit(solution)/shard_map/pallas_call | solution.py:47
  85.2 18.4 %all_to_all.56.arrived_ref = f32[8,128,256]{2,1,0:T(8,128)S(1)} all-to-all(f32[8,128,256]{2,1,0:T(8,128)S(1)} %get-tuple-element.27.last_ref), channel_id=1, replica_groups=mesh['x'=4,'yh'=2,'yl'=2,'z'=8,'core'=2] {'x','yh'}, dimensions={0} | all-to-all | bytes 2097152 | tf_op jit(solution)/shard_map/all_to_all | solution.py:32
  103.8 27.7 %all_to_all.57.own_ref = bf16[16,128,256]{2,1,0:T(8,128)(2,1)S(1)} all-to-all(bf16[16,128,256]{2,1,0:T(8,128)(2,1)S(1)} %get-tuple-element.31), channel_id=1, replica_groups=mesh['x'=4,'yh'=2,'yl'=2,'z'=8,'core'=2] {'yl','z'}, dimensions={0} | all-to-all | bytes 2097152 | tf_op jit(solution)/shard_map/all_to_all | solution.py:32
  131.5 3.4 %collective-permute-start.5 = (bf16[16,128,256]{2,1,0:T(8,128)(2,1)S(1)}, bf16[16,128,256]{2,1,0:T(8,128)(2,1)S(1)}, u32[]{:S(2)}, u32[]{:S(2)}) collective-permute-start(bf16[16,128,256]{2,1,0:T(8,128)(2,1)S(1)} %all_to_all.57.own_ref), channel_id=1, source_target_pairs={{0,1},{1,0},{2,3},{3,2},{4,5},{5,4},{6,7},{7,6},{8,9},{9,8},{10,11... | collective-permute-start | bytes 3145736 | tf_op jit(solution)/shard_map/ppermute | solution.py:314
  134.9 2.3 collective-permute-done.5.other_ref
  137.2 4.7 %shard_map.64 = f32[8,128,256]{2,1,0:T(8,128)S(1)} custom-call(s32[48]{0:T(128)S(1)} %get-tuple-element.42.source_ref, s32[48]{0:T(128)S(1)} %get-tuple-element.47.target_ref, bf16[48,256,256]{2,1,0:T(8,128)(2,1)} %tiles_ref.7, bf16[16,128,256]{2,1,0:T(8,128)(2,1)S(1)} %all_to_all.57.own_ref, bf16[16,128,256]{2,1,0:T(8,128)(2,1)S(1)} %collective-permute-done.5.other_ref, ...), custom_call_target="tpu_custom_call" | custom-call | tf_op jit(solution)/shard_map/pallas_call | solution.py:47
  141.9 20.2 %all_to_all.58.arrived_ref = f32[8,128,256]{2,1,0:T(8,128)S(1)} all-to-all(f32[8,128,256]{2,1,0:T(8,128)S(1)} %shard_map.64), channel_id=1, replica_groups=mesh['x'=4,'yh'=2,'yl'=2,'z'=8,'core'=2] {'x','yh'}, dimensions={0} | all-to-all | bytes 2097152 | tf_op jit(solution)/shard_map/all_to_all | solution.py:32
  162.4 12.8 %all_to_all.59.in_ref = f32[32,1,896]{2,1,0:T(1,128)S(1)} all-to-all(f32[32,1,896]{2,1,0:T(1,128)S(1)} %get-tuple-element.33), channel_id=1, replica_groups=mesh['x'=4,'yh'=2,'yl'=2,'z'=8,'core'=2] {'x','yh','yl','core'}, dimensions={0} | all-to-all | bytes 229376 | tf_op jit(solution)/shard_map/all_to_all | solution.py:32
  175.4 10.7 %all_to_all.60.sums_ref = f32[8,1,896]{2,1,0:T(1,128)S(1)} all-to-all(f32[8,1,896]{2,1,0:T(1,128)S(1)} %shard_map.66), channel_id=1, replica_groups=mesh['x'=4,'yh'=2,'yl'=2,'z'=8,'core'=2] {'z'}, dimensions={0} | all-to-all | bytes 57344 | tf_op jit(solution)/shard_map/all_to_all | solution.py:32
  186.4 27.2 %all_to_all.61.own_ref = bf16[16,128,256]{2,1,0:T(8,128)(2,1)S(1)} all-to-all(bf16[16,128,256]{2,1,0:T(8,128)(2,1)S(1)} %get-tuple-element.35), channel_id=1, replica_groups=mesh['x'=4,'yh'=2,'yl'=2,'z'=8,'core'=2] {'yl','z'}, dimensions={0} | all-to-all | bytes 2097152 | tf_op jit(solution)/shard_map/all_to_all | solution.py:32
  213.6 2.7 %collective-permute-start.6 = (bf16[16,128,256]{2,1,0:T(8,128)(2,1)S(1)}, bf16[16,128,256]{2,1,0:T(8,128)(2,1)S(1)}, u32[]{:S(2)}, u32[]{:S(2)}) collective-permute-start(bf16[16,128,256]{2,1,0:T(8,128)(2,1)S(1)} %all_to_all.61.own_ref), channel_id=1, source_target_pairs={{0,1},{1,0},{2,3},{3,2},{4,5},{5,4},{6,7},{7,6},{8,9},{9,8},{10,11... | collective-permute-start | bytes 3145736 | tf_op jit(solution)/shard_map/ppermute | solution.py:314
  216.3 2.3 collective-permute-done.6.other_ref
  218.6 4.0 %shard_map.68 = f32[8,128,256]{2,1,0:T(8,128)S(1)} custom-call(s32[48]{0:T(128)S(1)} %get-tuple-element.42.source_ref, s32[48]{0:T(128)S(1)} %get-tuple-element.47.target_ref, bf16[48,256,256]{2,1,0:T(8,128)(2,1)} %tiles_ref.7, bf16[16,128,256]{2,1,0:T(8,128)(2,1)S(1)} %all_to_all.61.own_ref, bf16[16,128,256]{2,1,0:T(8,128)(2,1)S(1)} %collective-permute-done.6.other_ref), custom_call_target="tpu_custom_call" | custom-call | tf_op jit(solution)/shard_map/pallas_call | solution.py:47
  222.6 18.1 %all_to_all.62.arrived_ref = f32[8,128,256]{2,1,0:T(8,128)S(1)} all-to-all(f32[8,128,256]{2,1,0:T(8,128)S(1)} %shard_map.68), channel_id=1, replica_groups=mesh['x'=4,'yh'=2,'yl'=2,'z'=8,'core'=2] {'x','yh'}, dimensions={0} | all-to-all | bytes 2097152 | tf_op jit(solution)/shard_map/all_to_all | solution.py:32
  240.9 21.5 %all_to_all.63.sums_ref = f32[256,1,128]{2,1,0:T(1,128)S(1)} all-to-all(f32[256,1,128]{2,1,0:T(1,128)S(1)} %get-tuple-element.37), channel_id=1, replica_groups=mesh['x'=4,'yh'=2,'yl'=2,'z'=8,'core'=2] {'x','yh','yl','z','core'}, dimensions={0} | all-to-all | bytes 262144 | tf_op jit(solution)/shard_map/all_to_all | solution.py:32
  262.4 1.2 shard_map.70
  (17 shorter events, 1.5 us)
Async XLA Ops:
  0.6 45.6 %copy-start.1 = (s32[256]{0:T(256)S(1)}, s32[256]{0:T(256)}, u32[]{:S(2)}) copy-start(s32[256]{0:T(256)} %param.7) | copy-start | bytes 3076
  2.0 19.1 %all-to-all-start = ((s32[32,1,256]{2,1,0:T(1,128)}), s32[32,1,256]{2,1,0:T(1,128)S(1)}, u32[]{:S(2)}, u32[]{:S(2)}) async-start(s32[32,1,256]{2,1,0:T(1,128)} %broadcast_in_dim.12), calls=%async_computation | async-start | bytes 65536 | tf_op jit(solution)/shard_map/all_to_all | solution.py:32
  47.3 26.2 %all-to-all-start.2 = ((bf16[16,128,256]{2,1,0:T(8,128)(2,1)}), bf16[16,128,256]{2,1,0:T(8,128)(2,1)S(1)}, u32[]{:S(2)}, u32[]{:S(2)}) async-start(bf16[16,128,256]{2,1,0:T(8,128)(2,1)} %get-tuple-element.23), calls=%async_computation.2 | async-start | bytes 2097152 | tf_op jit(solution)/shard_map/all_to_all | solution.py:32
  51.1 3.7 %collective-permute-start = (f32[2,1,256]{2,1,0:T(1,128)S(1)}, f32[2,1,256]{2,1,0:T(1,128)S(1)}, u32[]{:S(2)}, u32[]{:S(2)}) collective-permute-start(f32[2,1,256]{2,1,0:T(1,128)S(1)} %get-tuple-element.44), channel_id=1, source_target_pairs={{0,64},{64,128},{128,192},{192,0},{1,65},{65,129},{129,193},{193,1... | collective-permute-start | bytes 6152 | tf_op jit(solution)/shard_map/ppermute | solution.py:291
  51.2 3.6 %collective-permute-start.2 = (f32[2,1,256]{2,1,0:T(1,128)S(1)}, f32[2,1,256]{2,1,0:T(1,128)S(1)}, u32[]{:S(2)}, u32[]{:S(2)}) collective-permute-start(f32[2,1,256]{2,1,0:T(1,128)S(1)} %get-tuple-element.45), channel_id=1, source_target_pairs={{0,192},{64,0},{128,64},{192,128},{1,193},{65,1},{129,65},{193,129... | collective-permute-start | bytes 6152 | tf_op jit(solution)/shard_map/ppermute | solution.py:291
  53.8 3.9 %collective-permute-start.1 = (f32[2,1,256]{2,1,0:T(1,128)S(1)}, f32[2,1,256]{2,1,0:T(1,128)S(1)}, u32[]{:S(2)}, u32[]{:S(2)}) collective-permute-start(f32[2,1,256]{2,1,0:T(1,128)S(1)} %get-tuple-element.46), channel_id=1, source_target_pairs={{0,128},{64,192},{128,0},{192,64},{1,129},{65,193},{129,1},{193,65... | collective-permute-start | bytes 6152 | tf_op jit(solution)/shard_map/ppermute | solution.py:291
  57.8 4.3 %collective-permute-start.3 = (f32[1,256]{1,0:T(1,128)S(1)}, f32[1,256]{1,0:T(1,128)S(1)}, u32[]{:S(2)}, u32[]{:S(2)}) collective-permute-start(f32[1,256]{1,0:T(1,128)S(1)} %fusion.4), channel_id=1, source_target_pairs={{0,32},{32,0},{1,33},{33,1},{2,34},{34,2},{3,35},{35,3},{4,36},{36... | collective-permute-start | bytes 3080 | tf_op jit(solution)/shard_map/ppermute | solution.py:293
  73.5 7.7 %collective-permute-start.4 = (bf16[16,128,256]{2,1,0:T(8,128)(2,1)S(1)}, bf16[16,128,256]{2,1,0:T(8,128)(2,1)S(1)}, u32[]{:S(2)}, u32[]{:S(2)}) collective-permute-start(bf16[16,128,256]{2,1,0:T(8,128)(2,1)S(1)} %get-tuple-element.25.own_ref), channel_id=1, source_target_pairs={{0,1},{1,0},{2,3},{3,2},{4,5},{5,4},{6,7},{7,6},{8,9},{9,8},{10,11... | collective-permute-start | bytes 3145736 | tf_op jit(solution)/shard_map/ppermute | solution.py:314
  85.2 52.0 %copy-start = (f32[8,128,256]{2,1,0:T(8,128)}, f32[8,128,256]{2,1,0:T(8,128)S(1)}, u32[]{:S(2)}) copy-start(f32[8,128,256]{2,1,0:T(8,128)S(1)} %get-tuple-element.27.last_ref) | copy-start | bytes 3145732
  131.5 5.7 %collective-permute-start.5 = (bf16[16,128,256]{2,1,0:T(8,128)(2,1)S(1)}, bf16[16,128,256]{2,1,0:T(8,128)(2,1)S(1)}, u32[]{:S(2)}, u32[]{:S(2)}) collective-permute-start(bf16[16,128,256]{2,1,0:T(8,128)(2,1)S(1)} %all_to_all.57.own_ref), channel_id=1, source_target_pairs={{0,1},{1,0},{2,3},{3,2},{4,5},{5,4},{6,7},{7,6},{8,9},{9,8},{10,11... | collective-permute-start | bytes 3145736 | tf_op jit(solution)/shard_map/ppermute | solution.py:314
  213.6 5.0 %collective-permute-start.6 = (bf16[16,128,256]{2,1,0:T(8,128)(2,1)S(1)}, bf16[16,128,256]{2,1,0:T(8,128)(2,1)S(1)}, u32[]{:S(2)}, u32[]{:S(2)}) collective-permute-start(bf16[16,128,256]{2,1,0:T(8,128)(2,1)S(1)} %all_to_all.61.own_ref), channel_id=1, source_target_pairs={{0,1},{1,0},{2,3},{3,2},{4,5},{5,4},{6,7},{7,6},{8,9},{9,8},{10,11... | collective-permute-start | bytes 3145736 | tf_op jit(solution)/shard_map/ppermute | solution.py:314

commit v5 on v4

--- a/solution.py
+++ b/solution.py
@@ -13,8 +13,8 @@
 ROW = ("x", "yh")
 COL = ("yl", "z", "core")
 CHIPS = ("yl", "z")
-NEAR = ("x", "yh", "yl", "core")
-FAR = ("z",)
+NEAR = ("x", "yh", "yl")
+FAR = ("z", "core")
 F32 = jnp.float32
 BF16 = jnp.bfloat16
 CHUNK = 16

time: 264 us -> 265 us (level)
  blocking collectives: 178 us -> 181 us
    all_to_all x9, blocking collectives: 178 us -> 181 us  [exchange(): return lax.all_to_all(blocks, axis, 0, 0, tiled=True)]
where the time goes in v5:
time: 265 us
  blocking collectives  181 us (68%)
  waiting for transfers between devices  31.7 us (12%)
  starting transfers between devices  29.9 us (11%)
  Pallas kernels  19.9 us (8%)
    all_to_all x9, blocking collectives, exchange(): return lax.all_to_all(blocks, axis, 0, 0, tiled=True)  181 us
    all_to_all x2, waiting for transfers between devices, exchange(): return lax.all_to_all(blocks, axis, 0, 0, tiled=True)  18.6 us
    pallas_call x4, Pallas kernels, apply_tiles(): pl.pallas_call(kernel, in_specs=[SMEM] * len(scalars) + [HBM] + [VMEM] *...  16.6 us
    all_to_all x2, starting transfers between devices, exchange(): return lax.all_to_all(blocks, axis, 0, 0, tiled=True)  14.8 us
    ppermute x3, starting transfers between devices, other_core(): return lax.ppermute(own, 'core', [(0, 1), (1, 0)])  10.3 us
    ppermute x3, waiting for transfers between devices, other_core(): return lax.ppermute(own, 'core', [(0, 1), (1, 0)])  6.86 us
  transfers between devices with their start and end apart: 9, of which 8 were waited for; matrix products, arithmetic and copies ran while one was open for 0% of the time, Pallas kernels for 0%

profile of v5, /device:TPU:1, one launch (start us, length us, event | category | flops | bytes accessed | tf_op | source)
XLA Modules:
  0.0 264.9 jit_solution(17804926292914911157)
XLA Ops:
  0.6 1.4 broadcast_in_dim.12
  2.0 11.1 %all-to-all-start = ((s32[32,1,256]{2,1,0:T(1,128)}), s32[32,1,256]{2,1,0:T(1,128)S(1)}, u32[]{:S(2)}, u32[]{:S(2)}) async-start(s32[32,1,256]{2,1,0:T(1,128)} %broadcast_in_dim.12), calls=%async_computation | async-start | bytes 65536 | tf_op jit(solution)/shard_map/all_to_all | solution.py:32
  13.2 0.7 fusion.5
  13.9 7.2 %all-to-all-done.label_ref = s32[32,1,256]{2,1,0:T(1,128)S(1)} async-done(((s32[32,1,256]{2,1,0:T(1,128)}), s32[32,1,256]{2,1,0:T(1,128)S(1)}, u32[]{:S(2)}, u32[]{:S(2)}) %all-to-all-start) | async-done | bytes 32800 | tf_op jit(solution)/shard_map/all_to_all | solution.py:32
  21.1 4.0 %shard_map.59 = (f32[8,128,256]{2,1,0:T(8,128)S(1)}, f32[8,1,256]{2,1,0:T(1,128)S(1)}, f32[1,128]{1,0:T(1,128)S(1)}) custom-call(s32[48]{0:T(128)S(1)} %get-tuple-element.43.source_ref, s32[48]{0:T(128)S(1)} %get-tuple-element.47.target_ref, bf16[48,256,256]{2,1,0:T(8,128)(2,1)} %tiles_ref.7, s32[32,1,256]{2,1,0:T(1,128)S(1)} %all-to-all-done.label_ref), custom_call_target="tpu_custom_call" | custom-call | tf_op jit(solution)/shard_map/pallas_call | solution.py:47
  25.0 21.1 %all_to_all.55.arrived_ref = f32[8,128,256]{2,1,0:T(8,128)S(1)} all-to-all(f32[8,128,256]{2,1,0:T(8,128)S(1)} %get-tuple-element.22), channel_id=1, replica_groups=mesh['x'=4,'yh'=2,'yl'=2,'z'=8,'core'=2] {'x','yh'}, dimensions={0} | all-to-all | bytes 2097152 | tf_op jit(solution)/shard_map/all_to_all | solution.py:32
  46.2 1.1 shard_map.60
  47.3 3.7 %all-to-all-start.2 = ((bf16[16,128,256]{2,1,0:T(8,128)(2,1)}), bf16[16,128,256]{2,1,0:T(8,128)(2,1)S(1)}, u32[]{:S(2)}, u32[]{:S(2)}) async-start(bf16[16,128,256]{2,1,0:T(8,128)(2,1)} %get-tuple-element.23), calls=%async_computation.2 | async-start | bytes 2097152 | tf_op jit(solution)/shard_map/all_to_all | solution.py:32
  51.1 2.7 %collective-permute-start.2 = (f32[2,1,256]{2,1,0:T(1,128)S(1)}, f32[2,1,256]{2,1,0:T(1,128)S(1)}, u32[]{:S(2)}, u32[]{:S(2)}) collective-permute-start(f32[2,1,256]{2,1,0:T(1,128)S(1)} %get-tuple-element.45), channel_id=1, source_target_pairs={{0,192},{64,0},{128,64},{192,128},{1,193},{65,1},{129,65},{193,129... | collective-permute-start | bytes 6152 | tf_op jit(solution)/shard_map/ppermute | solution.py:291
  54.1 0.6 collective-permute-done
  54.8 3.0 %collective-permute-done.1 = f32[2,1,256]{2,1,0:T(1,128)S(1)} collective-permute-done((f32[2,1,256]{2,1,0:T(1,128)S(1)}, f32[2,1,256]{2,1,0:T(1,128)S(1)}, u32[]{:S(2)}, u32[]{:S(2)}) %collective-permute-start.1) | collective-permute-done | bytes 2080 | tf_op jit(solution)/shard_map/ppermute | solution.py:291
  57.8 1.7 collective-permute-start.3
  59.5 2.6 collective-permute-done.3
  62.1 11.4 %all-to-all-done.2.own_ref = bf16[16,128,256]{2,1,0:T(8,128)(2,1)S(1)} async-done(((bf16[16,128,256]{2,1,0:T(8,128)(2,1)}), bf16[16,128,256]{2,1,0:T(8,128)(2,1)S(1)}, u32[]{:S(2)}, u32[]{:S(2)}) %all-to-all-start.2) | async-done | bytes 1048608 | tf_op jit(solution)/shard_map/all_to_all | solution.py:32
  73.5 5.4 %collective-permute-start.4 = (bf16[16,128,256]{2,1,0:T(8,128)(2,1)S(1)}, bf16[16,128,256]{2,1,0:T(8,128)(2,1)S(1)}, u32[]{:S(2)}, u32[]{:S(2)}) collective-permute-start(bf16[16,128,256]{2,1,0:T(8,128)(2,1)S(1)} %get-tuple-element.25.own_ref), channel_id=1, source_target_pairs={{0,1},{1,0},{2,3},{3,2},{4,5},{5,4},{6,7},{7,6},{8,9},{9,8},{10,11... | collective-permute-start | bytes 3145736 | tf_op jit(solution)/shard_map/ppermute | solution.py:314
  78.9 2.3 collective-permute-done.4.other_ref
  81.2 4.0 %shard_map.62 = (f32[8,128,256]{2,1,0:T(8,128)S(1)}, f32[1,128]{1,0:T(1,128)S(1)}) custom-call(s32[48]{0:T(128)S(1)} %get-tuple-element.42.source_ref, s32[48]{0:T(128)S(1)} %get-tuple-element.47.target_ref, bf16[48,256,256]{2,1,0:T(8,128)(2,1)} %tiles_ref.7, bf16[16,128,256]{2,1,0:T(8,128)(2,1)S(1)} %get-tuple-element.25.own_ref, ...), custom_call_target="tpu_custom_call" | custom-call | tf_op jit(solution)/shard_map/pallas_call | solution.py:47
  85.2 18.4 %all_to_all.56.arrived_ref = f32[8,128,256]{2,1,0:T(8,128)S(1)} all-to-all(f32[8,128,256]{2,1,0:T(8,128)S(1)} %get-tuple-element.27.last_ref), channel_id=1, replica_groups=mesh['x'=4,'yh'=2,'yl'=2,'z'=8,'core'=2] {'x','yh'}, dimensions={0} | all-to-all | bytes 2097152 | tf_op jit(solution)/shard_map/all_to_all | solution.py:32
  103.8 27.8 %all_to_all.57.own_ref = bf16[16,128,256]{2,1,0:T(8,128)(2,1)S(1)} all-to-all(bf16[16,128,256]{2,1,0:T(8,128)(2,1)S(1)} %get-tuple-element.31), channel_id=1, replica_groups=mesh['x'=4,'yh'=2,'yl'=2,'z'=8,'core'=2] {'yl','z'}, dimensions={0} | all-to-all | bytes 2097152 | tf_op jit(solution)/shard_map/all_to_all | solution.py:32
  131.5 3.4 %collective-permute-start.5 = (bf16[16,128,256]{2,1,0:T(8,128)(2,1)S(1)}, bf16[16,128,256]{2,1,0:T(8,128)(2,1)S(1)}, u32[]{:S(2)}, u32[]{:S(2)}) collective-permute-start(bf16[16,128,256]{2,1,0:T(8,128)(2,1)S(1)} %all_to_all.57.own_ref), channel_id=1, source_target_pairs={{0,1},{1,0},{2,3},{3,2},{4,5},{5,4},{6,7},{7,6},{8,9},{9,8},{10,11... | collective-permute-start | bytes 3145736 | tf_op jit(solution)/shard_map/ppermute | solution.py:314
  134.9 2.3 collective-permute-done.5.other_ref
  137.2 4.7 %shard_map.64 = f32[8,128,256]{2,1,0:T(8,128)S(1)} custom-call(s32[48]{0:T(128)S(1)} %get-tuple-element.42.source_ref, s32[48]{0:T(128)S(1)} %get-tuple-element.47.target_ref, bf16[48,256,256]{2,1,0:T(8,128)(2,1)} %tiles_ref.7, bf16[16,128,256]{2,1,0:T(8,128)(2,1)S(1)} %all_to_all.57.own_ref, bf16[16,128,256]{2,1,0:T(8,128)(2,1)S(1)} %collective-permute-done.5.other_ref, ...), custom_call_target="tpu_custom_call" | custom-call | tf_op jit(solution)/shard_map/pallas_call | solution.py:47
  141.9 20.2 %all_to_all.58.arrived_ref = f32[8,128,256]{2,1,0:T(8,128)S(1)} all-to-all(f32[8,128,256]{2,1,0:T(8,128)S(1)} %shard_map.64), channel_id=1, replica_groups=mesh['x'=4,'yh'=2,'yl'=2,'z'=8,'core'=2] {'x','yh'}, dimensions={0} | all-to-all | bytes 2097152 | tf_op jit(solution)/shard_map/all_to_all | solution.py:32
  162.4 10.3 %all_to_all.59.in_ref = f32[16,1,896]{2,1,0:T(1,128)S(1)} all-to-all(f32[16,1,896]{2,1,0:T(1,128)S(1)} %get-tuple-element.33), channel_id=1, replica_groups=mesh['x'=4,'yh'=2,'yl'=2,'z'=8,'core'=2] {'x','yh','yl'}, dimensions={0} | all-to-all | bytes 114688 | tf_op jit(solution)/shard_map/all_to_all | solution.py:32
  172.7 14.3 %all_to_all.60.sums_ref = f32[16,1,896]{2,1,0:T(1,128)S(1)} all-to-all(f32[16,1,896]{2,1,0:T(1,128)S(1)} %shard_map.66), channel_id=1, replica_groups=mesh['x'=4,'yh'=2,'yl'=2,'z'=8,'core'=2] {'z','core'}, dimensions={0} | all-to-all | bytes 114688 | tf_op jit(solution)/shard_map/all_to_all | solution.py:32
  187.4 28.7 %all_to_all.61.own_ref = bf16[16,128,256]{2,1,0:T(8,128)(2,1)S(1)} all-to-all(bf16[16,128,256]{2,1,0:T(8,128)(2,1)S(1)} %get-tuple-element.35), channel_id=1, replica_groups=mesh['x'=4,'yh'=2,'yl'=2,'z'=8,'core'=2] {'yl','z'}, dimensions={0} | all-to-all | bytes 2097152 | tf_op jit(solution)/shard_map/all_to_all | solution.py:32
  216.1 1.5 collective-permute-start.6
  217.6 2.3 collective-permute-done.6.other_ref
  219.8 4.0 %shard_map.68 = f32[8,128,256]{2,1,0:T(8,128)S(1)} custom-call(s32[48]{0:T(128)S(1)} %get-tuple-element.42.source_ref, s32[48]{0:T(128)S(1)} %get-tuple-element.47.target_ref, bf16[48,256,256]{2,1,0:T(8,128)(2,1)} %tiles_ref.7, bf16[16,128,256]{2,1,0:T(8,128)(2,1)S(1)} %all_to_all.61.own_ref, bf16[16,128,256]{2,1,0:T(8,128)(2,1)S(1)} %collective-permute-done.6.other_ref), custom_call_target="tpu_custom_call" | custom-call | tf_op jit(solution)/shard_map/pallas_call | solution.py:47
  223.8 18.4 %all_to_all.62.arrived_ref = f32[8,128,256]{2,1,0:T(8,128)S(1)} all-to-all(f32[8,128,256]{2,1,0:T(8,128)S(1)} %shard_map.68), channel_id=1, replica_groups=mesh['x'=4,'yh'=2,'yl'=2,'z'=8,'core'=2] {'x','yh'}, dimensions={0} | all-to-all | bytes 2097152 | tf_op jit(solution)/shard_map/all_to_all | solution.py:32
  242.5 21.2 %all_to_all.63.sums_ref = f32[256,1,128]{2,1,0:T(1,128)S(1)} all-to-all(f32[256,1,128]{2,1,0:T(1,128)S(1)} %get-tuple-element.37), channel_id=1, replica_groups=mesh['x'=4,'yh'=2,'yl'=2,'z'=8,'core'=2] {'x','yh','yl','z','core'}, dimensions={0} | all-to-all | bytes 262144 | tf_op jit(solution)/shard_map/all_to_all | solution.py:32
  263.7 1.2 shard_map.70
  (17 shorter events, 1.5 us)
Async XLA Ops:
  0.6 45.6 %copy-start.1 = (s32[256]{0:T(256)S(1)}, s32[256]{0:T(256)}, u32[]{:S(2)}) copy-start(s32[256]{0:T(256)} %param.7) | copy-start | bytes 3076
  2.0 19.1 %all-to-all-start = ((s32[32,1,256]{2,1,0:T(1,128)}), s32[32,1,256]{2,1,0:T(1,128)S(1)}, u32[]{:S(2)}, u32[]{:S(2)}) async-start(s32[32,1,256]{2,1,0:T(1,128)} %broadcast_in_dim.12), calls=%async_computation | async-start | bytes 65536 | tf_op jit(solution)/shard_map/all_to_all | solution.py:32
  47.3 26.2 %all-to-all-start.2 = ((bf16[16,128,256]{2,1,0:T(8,128)(2,1)}), bf16[16,128,256]{2,1,0:T(8,128)(2,1)S(1)}, u32[]{:S(2)}, u32[]{:S(2)}) async-start(bf16[16,128,256]{2,1,0:T(8,128)(2,1)} %get-tuple-element.23), calls=%async_computation.2 | async-start | bytes 2097152 | tf_op jit(solution)/shard_map/all_to_all | solution.py:32
  51.0 3.7 %collective-permute-start = (f32[2,1,256]{2,1,0:T(1,128)S(1)}, f32[2,1,256]{2,1,0:T(1,128)S(1)}, u32[]{:S(2)}, u32[]{:S(2)}) collective-permute-start(f32[2,1,256]{2,1,0:T(1,128)S(1)} %get-tuple-element.44), channel_id=1, source_target_pairs={{0,64},{64,128},{128,192},{192,0},{1,65},{65,129},{129,193},{193,1... | collective-permute-start | bytes 6152 | tf_op jit(solution)/shard_map/ppermute | solution.py:291
  51.1 3.6 %collective-permute-start.2 = (f32[2,1,256]{2,1,0:T(1,128)S(1)}, f32[2,1,256]{2,1,0:T(1,128)S(1)}, u32[]{:S(2)}, u32[]{:S(2)}) collective-permute-start(f32[2,1,256]{2,1,0:T(1,128)S(1)} %get-tuple-element.45), channel_id=1, source_target_pairs={{0,192},{64,0},{128,64},{192,128},{1,193},{65,1},{129,65},{193,129... | collective-permute-start | bytes 6152 | tf_op jit(solution)/shard_map/ppermute | solution.py:291
  53.8 3.9 %collective-permute-start.1 = (f32[2,1,256]{2,1,0:T(1,128)S(1)}, f32[2,1,256]{2,1,0:T(1,128)S(1)}, u32[]{:S(2)}, u32[]{:S(2)}) collective-permute-start(f32[2,1,256]{2,1,0:T(1,128)S(1)} %get-tuple-element.46), channel_id=1, source_target_pairs={{0,128},{64,192},{128,0},{192,64},{1,129},{65,193},{129,1},{193,65... | collective-permute-start | bytes 6152 | tf_op jit(solution)/shard_map/ppermute | solution.py:291
  57.8 4.3 %collective-permute-start.3 = (f32[1,256]{1,0:T(1,128)S(1)}, f32[1,256]{1,0:T(1,128)S(1)}, u32[]{:S(2)}, u32[]{:S(2)}) collective-permute-start(f32[1,256]{1,0:T(1,128)S(1)} %fusion.4), channel_id=1, source_target_pairs={{0,32},{32,0},{1,33},{33,1},{2,34},{34,2},{3,35},{35,3},{4,36},{36... | collective-permute-start | bytes 3080 | tf_op jit(solution)/shard_map/ppermute | solution.py:293
  73.5 7.7 %collective-permute-start.4 = (bf16[16,128,256]{2,1,0:T(8,128)(2,1)S(1)}, bf16[16,128,256]{2,1,0:T(8,128)(2,1)S(1)}, u32[]{:S(2)}, u32[]{:S(2)}) collective-permute-start(bf16[16,128,256]{2,1,0:T(8,128)(2,1)S(1)} %get-tuple-element.25.own_ref), channel_id=1, source_target_pairs={{0,1},{1,0},{2,3},{3,2},{4,5},{5,4},{6,7},{7,6},{8,9},{9,8},{10,11... | collective-permute-start | bytes 3145736 | tf_op jit(solution)/shard_map/ppermute | solution.py:314
  85.2 52.0 %copy-start = (f32[8,128,256]{2,1,0:T(8,128)}, f32[8,128,256]{2,1,0:T(8,128)S(1)}, u32[]{:S(2)}) copy-start(f32[8,128,256]{2,1,0:T(8,128)S(1)} %get-tuple-element.27.last_ref) | copy-start | bytes 3145732
  131.5 5.7 %collective-permute-start.5 = (bf16[16,128,256]{2,1,0:T(8,128)(2,1)S(1)}, bf16[16,128,256]{2,1,0:T(8,128)(2,1)S(1)}, u32[]{:S(2)}, u32[]{:S(2)}) collective-permute-start(bf16[16,128,256]{2,1,0:T(8,128)(2,1)S(1)} %all_to_all.57.own_ref), channel_id=1, source_target_pairs={{0,1},{1,0},{2,3},{3,2},{4,5},{5,4},{6,7},{7,6},{8,9},{9,8},{10,11... | collective-permute-start | bytes 3145736 | tf_op jit(solution)/shard_map/ppermute | solution.py:314
  216.1 3.8 %collective-permute-start.6 = (bf16[16,128,256]{2,1,0:T(8,128)(2,1)S(1)}, bf16[16,128,256]{2,1,0:T(8,128)(2,1)S(1)}, u32[]{:S(2)}, u32[]{:S(2)}) collective-permute-start(bf16[16,128,256]{2,1,0:T(8,128)(2,1)S(1)} %all_to_all.61.own_ref), channel_id=1, source_target_pairs={{0,1},{1,0},{2,3},{3,2},{4,5},{5,4},{6,7},{7,6},{8,9},{9,8},{10,11... | collective-permute-start | bytes 3145736 | tf_op jit(solution)/shard_map/ppermute | solution.py:314
